TPU v7x, 32 devices: a whole 2x2x4 slice. The times are simulated.
32 devices in a mesh: expert: 8 (over z, y), shard: 4 (over x, core).
Axes of the slice: x: 2, y: 2, z: 4, core: 2. Of those that a mesh axis runs over, the one named last changes fastest.
Arguments:
- images: bfloat16 [128, 197, 512], P(('expert', 'shard')), may hold values from -26 to 26
- attention_in: bfloat16 [512, 1536], P('shard'), may hold values from -0.25 to 0.25
- attention_out: bfloat16 [512, 512], P('shard'), may hold values from -0.75 to 0.75
- layer_gain: bfloat16 [2, 512], P(None, 'shard'), may hold values from 0.099609375 to 1.8984375
- layer_shift: bfloat16 [2, 512], P(None, 'shard'), may hold values from -3 to 3
- attention_bias: bfloat16 [3, 512], P(None, 'shard'), may hold values from -3 to 3
- expert_up: bfloat16 [8, 512, 2048], P('expert'), may hold values from -0.25 to 0.25
- hidden_bias: bfloat16 [8, 2048], P('expert'), may hold values from -3 to 3
- expert_down: bfloat16 [8, 2048, 512], P('expert'), may hold values from -0.1875 to 0.1875
- expert_bias: bfloat16 [8, 512], P('expert'), may hold values from -3 to 3
- routes: int32 [128, 197, 2], P(('expert', 'shard')), may hold values from 0 to 7, all different within a row; in each aligned block of 788 rows (0 to 787, 788 to 1575, ..., all dimensions but the last counted through in order) at most 394 rows name the same one
- gates: float32 [128, 197, 2], P(('expert', 'shard')), may hold values from 0.1 to 1
- cotangent: bfloat16 [128, 197, 512], P(('expert', 'shard')), may hold values from -6 to 6
Outputs:
- block_output: bfloat16 [128, 197, 512], P(('expert', 'shard'))
- gradient_images: float32 [128, 197, 512], P(('expert', 'shard'))
- gradient_attention_in: float32 [512, 1536], P('shard')
- gradient_attention_out: float32 [512, 512], P('shard')
- gradient_layer_gain: float32 [2, 512], P(None, 'shard')
- gradient_layer_shift: float32 [2, 512], P(None, 'shard')
- gradient_attention_bias: float32 [3, 512], P(None, 'shard')
- gradient_expert_up: float32 [8, 512, 2048], P('expert')
- gradient_hidden_bias: float32 [8, 2048], P('expert')
- gradient_expert_down: float32 [8, 2048, 512], P('expert')
- gradient_expert_bias: float32 [8, 512], P('expert')
- gradient_gates: float32 [128, 197, 2], P(('expert', 'shard'))
- stream_magnitude: float32 [3], replicated
Inputs may be any that keep to these rules, and one draw needn't show every extreme that they name: `routes`: the 2 experts of a token differ; among the tokens of one device no expert is named more than 394 times, and in every draw some device names some expert exactly 394 times.
All inputs are finite; a program needn't handle non-finite values.
Results may differ from a plain program's by a relative error of at most 0.019.
Values may be sent and summed in bfloat16 or wider, within the bound.
A program may use at most 128 MiB of HBM per device.

v0:
```python
import math

import jax
import jax.numpy as jnp
from jax import lax
from jax.sharding import PartitionSpec as P

HEADS = 8
HEAD = 64
TOP = 2


EPSILON = 1e-06
source_groups = 4
contract_rows = (((0,), (0,)), ((), ()))
contract_cols = (((1,), (1,)), ((), ()))


def normalize(values):
    centre = values - jnp.mean(values, axis=-1, keepdims=True)
    inverse = lax.rsqrt(jnp.mean(centre * centre, axis=-1, keepdims=True) + EPSILON)
    return (centre * inverse, inverse)


def normalize_back(incoming, unit, inverse, weight):
    scaled = incoming * weight
    first_mean = jnp.mean(scaled, axis=-1, keepdims=True)
    second_mean = jnp.mean(scaled * unit, axis=-1, keepdims=True)
    return inverse * (scaled - first_mean - unit * second_mean)


def exact_gelu(values):
    return jax.nn.gelu(values, approximate=False)


def local(
    images,
    attention_in,
    attention_out,
    layer_gain,
    layer_shift,
    attention_bias,
    expert_up,
    hidden_bias,
    expert_down,
    expert_bias,
    routes,
    gates,
    cotangent,
):
    image_count, image_tokens, model_width = images.shape
    tokens = image_count * image_tokens
    full_in, full_out, full_gain, full_shift, full_bias = (
        lax.all_gather(attention_in, "shard", axis=0, tiled=True),
        lax.all_gather(attention_out, "shard", axis=0, tiled=True),
        lax.all_gather(layer_gain, "shard", axis=1, tiled=True),
        lax.all_gather(layer_shift, "shard", axis=1, tiled=True),
        lax.all_gather(attention_bias, "shard", axis=1, tiled=True),
    )
    gain_rows = full_gain.astype(jnp.float32)
    shift_rows = full_shift.astype(jnp.float32)
    bias_rows = full_bias.astype(jnp.float32)
    stream = images.reshape(tokens, model_width).astype(jnp.float32)
    unit_one, inverse_one = normalize(stream)
    normed_one = (unit_one * gain_rows[0] + shift_rows[0]).astype(jnp.bfloat16)
    projected = jnp.dot(normed_one, full_in, preferred_element_type=jnp.float32)
    shape_four = (image_count, image_tokens, HEADS, HEAD)
    queries = (projected[:, :model_width] + bias_rows[0]).astype(jnp.bfloat16).reshape(shape_four)
    key_rows = projected[:, model_width : 2 * model_width].astype(jnp.bfloat16).reshape(shape_four)
    values = (
        (projected[:, 2 * model_width :] + bias_rows[1]).astype(jnp.bfloat16).reshape(shape_four)
    )
    score_scale = 1.0 / math.sqrt(HEAD)
    scores = (
        jnp.einsum("bqhd,bkhd->bhqk", queries, key_rows, preferred_element_type=jnp.float32)
        * score_scale
    )
    highest = jnp.max(scores, axis=-1, keepdims=True)
    powers = jnp.exp(scores - highest)
    totals = jnp.sum(powers, axis=-1, keepdims=True)
    softmax_rows = powers / totals
    log_total = highest + jnp.log(totals)
    context = (
        jnp.einsum(
            "bhqk,bkhd->bqhd",
            softmax_rows.astype(jnp.bfloat16),
            values,
            preferred_element_type=jnp.float32,
        )
        .reshape(tokens, model_width)
        .astype(jnp.bfloat16)
    )
    middle = stream + jnp.dot(context, full_out, preferred_element_type=jnp.float32) + bias_rows[2]
    unit_two, inverse_two = normalize(middle)
    normed_two = (unit_two * gain_rows[1] + shift_rows[1]).astype(jnp.bfloat16)
    experts_count = lax.axis_size("expert")
    capacity = max(2, 4 * tokens // experts_count)
    pair_expert = routes.reshape(tokens * TOP)
    labels = jnp.arange(experts_count, dtype=jnp.int32)
    onehot = (pair_expert[:, None] == labels[None, :]).astype(jnp.int32)
    position = jnp.sum((jnp.cumsum(onehot, axis=0) - onehot) * onehot, axis=1)
    slot_index = pair_expert * capacity + position
    paired_rows = jnp.broadcast_to(normed_two[:, None, :], (tokens, TOP, model_width)).reshape(
        tokens * TOP, model_width
    )
    empty_slots = jnp.zeros((experts_count * capacity, model_width), jnp.bfloat16)
    send_rows = (
        empty_slots.at[slot_index].set(paired_rows).reshape(experts_count, capacity, model_width)
    )
    up_matrix = expert_up[0]
    down_matrix = expert_down[0]
    hidden_shift = hidden_bias[0].astype(jnp.float32)
    output_shift = expert_bias[0].astype(jnp.float32)
    hidden_units = up_matrix.shape[1]
    received = lax.all_to_all(send_rows, "expert", split_axis=0, concat_axis=0, tiled=True)
    sources, slot_count, row_width = received.shape
    grouped = received.reshape(source_groups, sources // source_groups * slot_count, row_width)

    def one_block(row_block):
        hidden = jnp.dot(row_block, up_matrix, preferred_element_type=jnp.float32) + hidden_shift
        active = exact_gelu(hidden).astype(jnp.bfloat16)
        return (
            jnp.dot(active, down_matrix, preferred_element_type=jnp.float32) + output_shift
        ).astype(jnp.bfloat16)

    produced = lax.map(one_block, grouped).reshape(sources, slot_count, row_width)
    returned = lax.all_to_all(produced, "expert", split_axis=0, concat_axis=0, tiled=True)
    returned, kept_rows = (returned, received)
    pair_out = returned.reshape(experts_count * capacity, model_width)[slot_index].reshape(
        tokens, TOP, model_width
    )
    gate_rows = gates.reshape(tokens, TOP)
    pair_float = pair_out.astype(jnp.float32)
    block_stream = middle + jnp.sum(pair_float * gate_rows[:, :, None], axis=1)
    block_output = block_stream.astype(jnp.bfloat16).reshape(image_count, image_tokens, model_width)
    local_squares = jnp.stack(
        [jnp.sum(stream * stream), jnp.sum(middle * middle), jnp.sum(block_stream * block_stream)]
    )
    total_squares = lax.psum(local_squares, ("expert", "shard"))
    entries = float(tokens * model_width * experts_count * lax.axis_size("shard"))
    magnitude = jnp.sqrt(total_squares / entries)
    upstream = cotangent.reshape(tokens, model_width).astype(jnp.float32)
    gradient_gates = jnp.sum(upstream[:, None, :] * pair_float, axis=2).reshape(
        image_count, image_tokens, TOP
    )
    pair_grads = (
        (gate_rows[:, :, None] * upstream[:, None, :])
        .astype(jnp.bfloat16)
        .reshape(tokens * TOP, model_width)
    )
    send_grads = (
        empty_slots.at[slot_index].set(pair_grads).reshape(experts_count, capacity, model_width)
    )
    incoming_grads = lax.all_to_all(send_grads, "expert", split_axis=0, concat_axis=0, tiled=True)
    rows_split = kept_rows.reshape(source_groups, -1, model_width)
    grads_split = incoming_grads.reshape(source_groups, -1, model_width)

    def expert_back(running, block_pair):
        row_block, incoming = block_pair
        sum_up, sum_hidden, sum_down, sum_output = running
        hidden = jnp.dot(row_block, up_matrix, preferred_element_type=jnp.float32) + hidden_shift
        active, gelu_back = jax.vjp(exact_gelu, hidden)
        active_low = active.astype(jnp.bfloat16)
        back_active = lax.dot_general(
            incoming, down_matrix, contract_cols, preferred_element_type=jnp.float32
        )
        back_hidden = gelu_back(back_active)[0].astype(jnp.bfloat16)
        sum_up = sum_up + lax.dot_general(
            row_block, back_hidden, contract_rows, preferred_element_type=jnp.float32
        )
        sum_hidden = sum_hidden + jnp.sum(back_hidden, axis=0, dtype=jnp.float32)
        sum_down = sum_down + lax.dot_general(
            active_low, incoming, contract_rows, preferred_element_type=jnp.float32
        )
        sum_output = sum_output + jnp.sum(incoming, axis=0, dtype=jnp.float32)
        back_rows = lax.dot_general(
            back_hidden, up_matrix, contract_cols, preferred_element_type=jnp.float32
        ).astype(jnp.bfloat16)
        return ((sum_up, sum_hidden, sum_down, sum_output), back_rows)

    starting = (
        jnp.zeros((model_width, hidden_units), jnp.float32),
        jnp.zeros((hidden_units,), jnp.float32),
        jnp.zeros((hidden_units, model_width), jnp.float32),
        jnp.zeros((model_width,), jnp.float32),
    )
    expert_sums, back_rows = lax.scan(expert_back, starting, (rows_split, grads_split))
    up_local, hidden_local, down_local, output_local = expert_sums
    up_total, hidden_total, down_total, output_total = (
        lax.psum(up_local.astype(jnp.bfloat16), "shard").astype(jnp.float32),
        lax.psum(hidden_local.astype(jnp.bfloat16), "shard").astype(jnp.float32),
        lax.psum(down_local.astype(jnp.bfloat16), "shard").astype(jnp.float32),
        lax.psum(output_local.astype(jnp.bfloat16), "shard").astype(jnp.float32),
    )
    routed_back = lax.all_to_all(
        back_rows.reshape(experts_count, capacity, model_width),
        "expert",
        split_axis=0,
        concat_axis=0,
        tiled=True,
    )
    back_pairs = routed_back.reshape(experts_count * capacity, model_width)[slot_index]
    back_normed_two = jnp.sum(
        back_pairs.reshape(tokens, TOP, model_width).astype(jnp.float32), axis=1
    )
    gain_two_grad = jnp.sum(back_normed_two * unit_two, axis=0)
    shift_two_grad = jnp.sum(back_normed_two, axis=0)
    back_middle = upstream + normalize_back(back_normed_two, unit_two, inverse_two, gain_rows[1])
    back_branch = back_middle.astype(jnp.bfloat16)
    out_bias_grad = jnp.sum(back_branch, axis=0, dtype=jnp.float32)
    out_weight_grad = lax.dot_general(
        context, back_branch, contract_rows, preferred_element_type=jnp.float32
    )
    back_context = (
        lax.dot_general(back_branch, full_out, contract_cols, preferred_element_type=jnp.float32)
        .astype(jnp.bfloat16)
        .reshape(shape_four)
    )
    again_scores = (
        jnp.einsum("bqhd,bkhd->bhqk", queries, key_rows, preferred_element_type=jnp.float32)
        * score_scale
    )
    recomputed = jnp.exp(again_scores - log_total)
    value_grad = jnp.einsum(
        "bhqk,bqhd->bkhd",
        recomputed.astype(jnp.bfloat16),
        back_context,
        preferred_element_type=jnp.float32,
    ).reshape(tokens, model_width)
    back_softmax = jnp.einsum(
        "bqhd,bkhd->bhqk", back_context, values, preferred_element_type=jnp.float32
    )
    shared = jnp.sum(back_softmax * recomputed, axis=-1, keepdims=True)
    back_scores = (recomputed * (back_softmax - shared)).astype(jnp.bfloat16)
    query_grad = (
        jnp.einsum(
            "bhqk,bkhd->bqhd", back_scores, key_rows, preferred_element_type=jnp.float32
        ).reshape(tokens, model_width)
        * score_scale
    )
    key_grad = (
        jnp.einsum(
            "bhqk,bqhd->bkhd", back_scores, queries, preferred_element_type=jnp.float32
        ).reshape(tokens, model_width)
        * score_scale
    )
    bias_grads = jnp.stack(
        [jnp.sum(query_grad, axis=0), jnp.sum(value_grad, axis=0), out_bias_grad]
    )
    back_projected = jnp.concatenate([query_grad, key_grad, value_grad], axis=1).astype(
        jnp.bfloat16
    )
    in_weight_grad = lax.dot_general(
        normed_one, back_projected, contract_rows, preferred_element_type=jnp.float32
    )
    back_normed_one = lax.dot_general(
        back_projected, full_in, contract_cols, preferred_element_type=jnp.float32
    )
    gradient_images = back_middle + normalize_back(
        back_normed_one, unit_one, inverse_one, gain_rows[0]
    )
    gain_grads = jnp.stack([jnp.sum(back_normed_one * unit_one, axis=0), gain_two_grad])
    shift_grads = jnp.stack([jnp.sum(back_normed_one, axis=0), shift_two_grad])
    owned_in, owned_out, owned_gain, owned_shift, owned_bias = (
        lax.psum_scatter(
            in_weight_grad.astype(jnp.bfloat16), "shard", scatter_dimension=0, tiled=True
        ).astype(jnp.float32),
        lax.psum_scatter(
            out_weight_grad.astype(jnp.bfloat16), "shard", scatter_dimension=0, tiled=True
        ).astype(jnp.float32),
        lax.psum_scatter(
            gain_grads.astype(jnp.bfloat16), "shard", scatter_dimension=1, tiled=True
        ).astype(jnp.float32),
        lax.psum_scatter(
            shift_grads.astype(jnp.bfloat16), "shard", scatter_dimension=1, tiled=True
        ).astype(jnp.float32),
        lax.psum_scatter(
            bias_grads.astype(jnp.bfloat16), "shard", scatter_dimension=1, tiled=True
        ).astype(jnp.float32),
    )
    summed_in, summed_out, summed_gain, summed_shift, summed_bias = (
        lax.psum(owned_in.astype(jnp.bfloat16), "expert").astype(jnp.float32),
        lax.psum(owned_out.astype(jnp.bfloat16), "expert").astype(jnp.float32),
        lax.psum(owned_gain.astype(jnp.bfloat16), "expert").astype(jnp.float32),
        lax.psum(owned_shift.astype(jnp.bfloat16), "expert").astype(jnp.float32),
        lax.psum(owned_bias.astype(jnp.bfloat16), "expert").astype(jnp.float32),
    )
    return (
        block_output,
        gradient_images.reshape(image_count, image_tokens, model_width),
        summed_in,
        summed_out,
        summed_gain,
        summed_shift,
        summed_bias,
        up_total[None],
        hidden_total[None],
        down_total[None],
        output_total[None],
        gradient_gates,
        magnitude,
    )


def solution(mesh):
    return jax.shard_map(
        local,
        mesh=mesh,
        in_specs=(
            P(("expert", "shard"), None, None),
            P("shard", None),
            P("shard", None),
            P(None, "shard"),
            P(None, "shard"),
            P(None, "shard"),
            P("expert", None, None),
            P("expert", None),
            P("expert", None, None),
            P("expert", None),
            P(("expert", "shard"), None, None),
            P(("expert", "shard"), None, None),
            P(("expert", "shard"), None, None),
        ),
        out_specs=(
            P(("expert", "shard"), None, None),
            P(("expert", "shard"), None, None),
            P("shard", None),
            P("shard", None),
            P(None, "shard"),
            P(None, "shard"),
            P(None, "shard"),
            P("expert", None, None),
            P("expert", None),
            P("expert", None, None),
            P("expert", None),
            P(("expert", "shard"), None, None),
            P(),
        ),
        check_vma=False,
    )
```

profile of v0, /device:TPU:0, one launch (start us, length us, event | category | flops | bytes accessed | tf_op | source)
XLA Modules:
  0.0 814.6 jit_solution(15276216687994963347)
XLA Ops:
  16.3 5.3 mul.251
  22.2 17.2 %scatter_custom_fusion.1 = bf16[3152,512]{1,0:T(8,128)(2,1)S(1)} fusion(s32[1576]{0:T(1024)S(1)} %fusion.94, f32[1576,512]{1,0:T(8,128)} %mul.251, f32[1576]{0:T(1024)S(1)} %mul.248, bf16[]{:T(256)} %constant.177.clone.1), kind=kCustom, calls=%fused_computation.144 | custom fusion | flops 1613824 | bytes 6463490 | tf_op jit(solution)/shard_map/scatter | solution.py:152
  41.5 7.7 all-to-all-start.2
  52.4 5.0 all_gather.15
  57.5 5.0 all_gather.16
  62.5 5.1 all_gather.18
  67.6 7.7 all_gather.19
  111.5 11.9 %scatter_custom_fusion = bf16[3152,512]{1,0:T(8,128)(2,1)S(1)} fusion(s32[1576]{0:T(1024)S(1)} %fusion.94, bf16[1576,512]{1,0:T(8,128)(2,1)} %reshape.293, bf16[]{:T(256)} %constant.177.clone.1), kind=kCustom, calls=%fused_computation.148 | custom fusion | bytes 3228160 | tf_op jit(solution)/shard_map/scatter | solution.py:108
  125.6 6.2 all-to-all-start
  135.4 70.5 %all-to-all-done = bf16[8,394,512]{2,1,0:T(8,128)(2,1)} async-done(((bf16[8,394,512]{2,1,0:T(8,128)(2,1)}), bf16[8,394,512]{2,1,0:T(8,128)(2,1)}, u32[]{:S(2)}, u32[]{:S(2)}) %all-to-all-start) | async-done | bytes 3227680 | tf_op jit(solution)/shard_map/all_to_all | solution.py:115
  205.9 4.5 reshape.254
  212.3 165.6 %while.30 = (s32[]{:T(128)}, f32[512,2048]{1,0:T(8,128)}, f32[2048]{0:T(1024)S(1)}, f32[2048,512]{1,0:T(8,128)}, f32[512]{0:T(512)S(1)}, /*index=5*/bf16[4,788,5...) while((s32[]{:T(128)}, f32[512,2048]{1,0:T(8,128)}, ...), condition=%wide.region_17.18_spmd.clone, body=%wide.region_14.17_spmd.clone.sunk | while | flops 8403747328 | bytes 170063632 | solution.py:187
  212.8 17.9 %fusion.153 = (f32[788,2048]{1,0:T(8,128)}, f32[788,2048]{1,0:T(8,128)}) fusion(f32[2048]{0:T(1024)S(1)} %get-tuple-element.471, bf16[512,2048]{1,0:T(8,128)(2,1)} %get-tuple-element.470, bf16[4,788,512]{2,1,0:T(8,128)(2,1)} %get-tuple-element.469, s32[]{:T(128)} %get-tuple-element.450), kind=kOutput, calls=%fused_computation.61.clone.1 | convolution fusion | flops 1754226688 | bytes 15827456 | tf_op jit(solution)/shard_map/while/body/eval_jaxpr/dot_general | solution.py:161
  230.7 9.4 %select_add_fusion.10 = f32[2048,512]{1,0:T(8,128)} fusion(f32[2048,512]{1,0:T(8,128)} %get-tuple-element.453, f32[788,2048]{1,0:T(8,128)} %get-tuple-element.409, f32[788,2048]{1,0:T(8,128)} %get-tuple-element.410, f32[2048]{0:T(1024)S(1)} %get-tuple-element.471, pred[]{:T(512)S(6)} %compare.4, bf16[4,788,512]{2,1,0:T(8,128)(2,1)S(1)} %get-tuple-element.472, ...), kind=kOutput, calls=%fused_computation.78.clone.1 | convolution fusion | flops 1661108224 | bytes 22118404 | tf_op jit(solution)/shard_map/while/body/eval_jaxpr/dot_general | solution.py:172
  240.1 5.7 convert_reduce_fusion.6
  245.8 4.4 select_add_fusion.8
  253.2 17.9 %fusion.153 = (f32[788,2048]{1,0:T(8,128)}, f32[788,2048]{1,0:T(8,128)}) fusion(f32[2048]{0:T(1024)S(1)} %get-tuple-element.471, bf16[512,2048]{1,0:T(8,128)(2,1)} %get-tuple-element.470, bf16[4,788,512]{2,1,0:T(8,128)(2,1)} %get-tuple-element.469, s32[]{:T(128)} %get-tuple-element.450), kind=kOutput, calls=%fused_computation.61.clone.1 | convolution fusion | flops 1754226688 | bytes 15827456 | tf_op jit(solution)/shard_map/while/body/eval_jaxpr/dot_general | solution.py:161
  271.1 10.6 %select_add_fusion.10 = f32[2048,512]{1,0:T(8,128)} fusion(f32[2048,512]{1,0:T(8,128)} %get-tuple-element.453, f32[788,2048]{1,0:T(8,128)} %get-tuple-element.409, f32[788,2048]{1,0:T(8,128)} %get-tuple-element.410, f32[2048]{0:T(1024)S(1)} %get-tuple-element.471, pred[]{:T(512)S(6)} %compare.4, bf16[4,788,512]{2,1,0:T(8,128)(2,1)S(1)} %get-tuple-element.472, ...), kind=kOutput, calls=%fused_computation.78.clone.1 | convolution fusion | flops 1661108224 | bytes 22118404 | tf_op jit(solution)/shard_map/while/body/eval_jaxpr/dot_general | solution.py:172
  281.7 5.7 convert_reduce_fusion.6
  287.4 4.4 select_add_fusion.8
  294.8 17.9 %fusion.153 = (f32[788,2048]{1,0:T(8,128)}, f32[788,2048]{1,0:T(8,128)}) fusion(f32[2048]{0:T(1024)S(1)} %get-tuple-element.471, bf16[512,2048]{1,0:T(8,128)(2,1)} %get-tuple-element.470, bf16[4,788,512]{2,1,0:T(8,128)(2,1)} %get-tuple-element.469, s32[]{:T(128)} %get-tuple-element.450), kind=kOutput, calls=%fused_computation.61.clone.1 | convolution fusion | flops 1754226688 | bytes 15827456 | tf_op jit(solution)/shard_map/while/body/eval_jaxpr/dot_general | solution.py:161
  312.7 10.6 %select_add_fusion.10 = f32[2048,512]{1,0:T(8,128)} fusion(f32[2048,512]{1,0:T(8,128)} %get-tuple-element.453, f32[788,2048]{1,0:T(8,128)} %get-tuple-element.409, f32[788,2048]{1,0:T(8,128)} %get-tuple-element.410, f32[2048]{0:T(1024)S(1)} %get-tuple-element.471, pred[]{:T(512)S(6)} %compare.4, bf16[4,788,512]{2,1,0:T(8,128)(2,1)S(1)} %get-tuple-element.472, ...), kind=kOutput, calls=%fused_computation.78.clone.1 | convolution fusion | flops 1661108224 | bytes 22118404 | tf_op jit(solution)/shard_map/while/body/eval_jaxpr/dot_general | solution.py:172
  323.3 5.7 convert_reduce_fusion.6
  336.4 17.9 %fusion.153 = (f32[788,2048]{1,0:T(8,128)}, f32[788,2048]{1,0:T(8,128)}) fusion(f32[2048]{0:T(1024)S(1)} %get-tuple-element.471, bf16[512,2048]{1,0:T(8,128)(2,1)} %get-tuple-element.470, bf16[4,788,512]{2,1,0:T(8,128)(2,1)} %get-tuple-element.469, s32[]{:T(128)} %get-tuple-element.450), kind=kOutput, calls=%fused_computation.61.clone.1 | convolution fusion | flops 1754226688 | bytes 15827456 | tf_op jit(solution)/shard_map/while/body/eval_jaxpr/dot_general | solution.py:161
  354.3 10.6 %select_add_fusion.10 = f32[2048,512]{1,0:T(8,128)} fusion(f32[2048,512]{1,0:T(8,128)} %get-tuple-element.453, f32[788,2048]{1,0:T(8,128)} %get-tuple-element.409, f32[788,2048]{1,0:T(8,128)} %get-tuple-element.410, f32[2048]{0:T(1024)S(1)} %get-tuple-element.471, pred[]{:T(512)S(6)} %compare.4, bf16[4,788,512]{2,1,0:T(8,128)(2,1)S(1)} %get-tuple-element.472, ...), kind=kOutput, calls=%fused_computation.78.clone.1 | convolution fusion | flops 1661108224 | bytes 22118404 | tf_op jit(solution)/shard_map/while/body/eval_jaxpr/dot_general | solution.py:172
  364.9 5.7 convert_reduce_fusion.6
  378.0 4.5 reshape.260
  382.5 4.5 all-to-all-start.3
  387.2 74.5 %while.29 = (s32[]{:T(128)}, bf16[4,788,512]{2,1,0:T(8,128)(2,1)S(1)}, bf16[4,788,512]{2,1,0:T(8,128)(2,1)}, bf16[512,2048]{1,0:T(8,128)(2,1)}, f32[2048]{0:T(10...) while((s32[]{:T(128)}, bf16[4,788,512]{2,1,0:T(8,128)(2,1)S(1)}, ...), condition=%wide.region_11.12_spmd, body=%wide.region_10.11_spmd.sunk | while | flops 3412430848 | bytes 5827669 | solution.py:126
  387.4 18.5 %fusion.145 = bf16[4,788,512]{2,1,0:T(8,128)(2,1)S(1)} fusion(bf16[4,788,512]{2,1,0:T(8,128)(2,1)S(1)} %get-tuple-element.422, s32[]{:T(128)} %get-tuple-element.421, bf16[2048,512]{1,0:T(8,128)(2,1)} %get-tuple-element.434, bf16[512,2048]{1,0:T(8,128)(2,1)} %get-tuple-element.432, f32[2048]{0:T(1024)S(1)} %get-tuple-element.433, ...), kind=kOutput, calls=%fused_computation.26.clone.1 | convolution fusion | flops 3412430848 | bytes 5827584 | tf_op jit(solution)/shard_map/while/body/eval_jaxpr/dot_general | solution.py:123
  405.9 18.5 %fusion.145 = bf16[4,788,512]{2,1,0:T(8,128)(2,1)S(1)} fusion(bf16[4,788,512]{2,1,0:T(8,128)(2,1)S(1)} %get-tuple-element.422, s32[]{:T(128)} %get-tuple-element.421, bf16[2048,512]{1,0:T(8,128)(2,1)} %get-tuple-element.434, bf16[512,2048]{1,0:T(8,128)(2,1)} %get-tuple-element.432, f32[2048]{0:T(1024)S(1)} %get-tuple-element.433, ...), kind=kOutput, calls=%fused_computation.26.clone.1 | convolution fusion | flops 3412430848 | bytes 5827584 | tf_op jit(solution)/shard_map/while/body/eval_jaxpr/dot_general | solution.py:123
  424.5 18.5 %fusion.145 = bf16[4,788,512]{2,1,0:T(8,128)(2,1)S(1)} fusion(bf16[4,788,512]{2,1,0:T(8,128)(2,1)S(1)} %get-tuple-element.422, s32[]{:T(128)} %get-tuple-element.421, bf16[2048,512]{1,0:T(8,128)(2,1)} %get-tuple-element.434, bf16[512,2048]{1,0:T(8,128)(2,1)} %get-tuple-element.432, f32[2048]{0:T(1024)S(1)} %get-tuple-element.433, ...), kind=kOutput, calls=%fused_computation.26.clone.1 | convolution fusion | flops 3412430848 | bytes 5827584 | tf_op jit(solution)/shard_map/while/body/eval_jaxpr/dot_general | solution.py:123
  443.0 18.5 %fusion.145 = bf16[4,788,512]{2,1,0:T(8,128)(2,1)S(1)} fusion(bf16[4,788,512]{2,1,0:T(8,128)(2,1)S(1)} %get-tuple-element.422, s32[]{:T(128)} %get-tuple-element.421, bf16[2048,512]{1,0:T(8,128)(2,1)} %get-tuple-element.434, bf16[512,2048]{1,0:T(8,128)(2,1)} %get-tuple-element.432, f32[2048]{0:T(1024)S(1)} %get-tuple-element.433, ...), kind=kOutput, calls=%fused_computation.26.clone.1 | convolution fusion | flops 3412430848 | bytes 5827584 | tf_op jit(solution)/shard_map/while/body/eval_jaxpr/dot_general | solution.py:123
  464.2 6.1 all-to-all-start.1
  479.6 6.0 gather_fusion.1
  485.6 4.9 reshape.272
  490.5 52.5 %all-to-all-done.1 = bf16[8,394,512]{2,1,0:T(8,128)(2,1)} async-done(((bf16[8,394,512]{2,1,0:T(8,128)(2,1)}), bf16[8,394,512]{2,1,0:T(8,128)(2,1)}, u32[]{:S(2)}, u32[]{:S(2)}) %all-to-all-start.1) | async-done | bytes 3227680 | tf_op jit(solution)/shard_map/all_to_all | solution.py:127
  545.3 6.0 gather_fusion
  551.4 4.9 reshape.270
  556.3 5.9 reduce_sum.244
  562.2 19.0 %multiply_reduce_fusion.2 = (f32[788,2]{1,0:T(8,128)}, f32[788,512]{1,0:T(8,128)S(1)}) fusion(f32[788,2,512]{2,1,0:T(2,128)} %reshape.270, f32[788,512]{1,0:T(8,128)S(1)} %copy-done.10, f32[788,2]{1,0:T(8,128)} %copy.124), kind=kLoop, calls=%fused_computation.115 | loop fusion | flops 2822616 | bytes 6467904 | tf_op jit(solution)/shard_map/reduce_sum | solution.py:143
  591.5 8.0 multiply_reduce_fusion
  599.6 4.5 multiply_convert_fusion.4
  631.7 10.1 %all-reduce.3 = (bf16[1,2048]{1,0:T(2,128)(2,1)S(1)}, bf16[1,512]{1,0:T(2,128)(2,1)S(1)}) all-reduce(bf16[1,2048]{1,0:T(2,128)(2,1)S(1)} %broadcast_in_dim.81, bf16[1,512]{1,0:T(2,128)(2,1)S(1)} %broadcast_in_dim.85), channel_id=1, replica_groups=mesh['expert'=8,'shard'=4] {'shard'}, use_global_device_ids=true, to_apply=%region_42.43 | all-reduce | flops 2560 | bytes 10240 | tf_op jit(solution)/shard_map/psum | solution.py:191
  662.8 38.6 %psum.79 = f32[3]{0:T(128)S(1)} all-reduce(f32[3]{0:T(128)S(1)} %pad_maximum_fusion.3), channel_id=1, replica_groups=mesh['expert'=8,'shard'=4] {'expert','shard'}, use_global_device_ids=true, to_apply=%region_49.50 | all-reduce | flops 3 | bytes 24 | tf_op jit(solution)/shard_map/psum | solution.py:139
  713.1 14.8 %reduce-scatter.20.cloned.1.call-done = bf16[128,3]{1,0:T(8,128)(2,1)} async-done(((bf16[512,3]{1,0:T(8,128)(2,1)}), bf16[128,3]{1,0:T(8,128)(2,1)}) %reduce-scatter.20.cloned.1.call-update) | async-done | bytes 784
  728.7 21.4 %all-reduce.1 = (bf16[2,128]{1,0:T(2,128)(2,1)S(1)}, bf16[2,128]{1,0:T(2,128)(2,1)S(1)}, bf16[3,128]{1,0:T(4,128)(2,1)S(1)}) all-reduce(bf16[2,128]{1,0:T(2,128)(2,1)S(1)} %copy.148, bf16[2,128]{1,0:T(2,128)(2,1)S(1)} %copy.150, bf16[3,128]{1,0:T(4,128)(2,1)S(1)} %copy.152), channel_id=1, replica_groups=mesh['expert'=8,'shard'=4] {'expert'}, use_global_device_ids=true, to_apply=%region_31.32 | all-reduce | flops 896 | bytes 3584 | tf_op jit(solution)/shard_map/psum | solution.py:284
  751.9 52.1 %all-reduce.8.cloned.1.call-done = (bf16[128,1536]{1,0:T(8,128)(2,1)}, bf16[128,512]{1,0:T(8,128)(2,1)}) async-done(((bf16[128,1536]{1,0:T(8,128)(2,1)}, bf16[128,512]{1,0:T(8,128)(2,1)}), (bf16[128,1536]{1,0:T(8,128)(2,1)}, bf16[128,512]{1,0:T(8,128)(2,1)})) %all-reduce.8.cloned.1.call-update) | async-done | bytes 524304 | tf_op jit(solution)/shard_map/psum | solution.py:282
  (360 shorter events, 169.9 us)
Async XLA Ops:
  7.2 68.2 %all-gather.2.cloned.1.call-start = ((), (), s32[]{:S(2)}) async-start(), calls=%async_computation.9 | async-start | bytes 1966080 | tf_op jit(solution)/shard_map/all_gather | solution.py:54
  13.5 8.1 copy-start.9
  22.2 89.3 %copy-start.54 = (s32[1576]{0:T(1024)}, s32[1576]{0:T(1024)S(1)}, u32[]{:S(2)}) copy-start(s32[1576]{0:T(1024)S(1)} %fusion.94) | copy-start | bytes 18916
  41.5 7.7 copy-start.22
  41.5 84.1 %all-to-all-start.2 = ((bf16[8,394,512]{2,1,0:T(8,128)(2,1)}), bf16[8,394,512]{2,1,0:T(8,128)(2,1)}, u32[]{:S(2)}, u32[]{:S(2)}) async-start(bf16[8,394,512]{2,1,0:T(8,128)(2,1)} %reshape.258), calls=%async_computation.2 | async-start | bytes 6553600 | tf_op jit(solution)/shard_map/all_to_all | solution.py:154
  49.5 8.0 copy-start.69
  49.5 13.0 %copy-start.67 = (bf16[3,128]{1,0:T(4,128)(2,1)S(1)}, bf16[3,128]{1,0:T(4,128)(2,1)}, u32[]{:S(2)}) copy-start(bf16[3,128]{1,0:T(4,128)(2,1)} %param.22) | copy-start | bytes 2308
  49.5 18.1 %copy-start.43 = (bf16[128,512]{1,0:T(8,128)(2,1)S(1)}, bf16[128,512]{1,0:T(8,128)(2,1)}, u32[]{:S(2)}) copy-start(bf16[128,512]{1,0:T(8,128)(2,1)} %param.19) | copy-start | bytes 393220
  52.1 26.2 %copy-start.56 = (f32[788]{0:T(1024)}, f32[788]{0:T(1024)S(1)}, u32[]{:S(2)}) copy-start(f32[788]{0:T(1024)S(1)} %rsqrt.20) | copy-start | bytes 9460
  52.2 26.1 %copy-start.58 = (f32[788]{0:T(1024)}, f32[788]{0:T(1024)S(1)}, u32[]{:S(2)}) copy-start(f32[788]{0:T(1024)S(1)} %div.38) | copy-start | bytes 9460
  52.4 54.2 %copy-start.13 = (f32[788,512]{1,0:T(8,128)}, f32[788,512]{1,0:T(8,128)S(1)}, u32[]{:S(2)}) copy-start(f32[788,512]{1,0:T(8,128)S(1)} %reshape.266) | copy-start | bytes 4841476
  75.3 32.5 %copy-start.50 = (f32[1,512]{1,0:T(1,128)}, f32[1,512]{1,0:T(1,128)S(1)}, u32[]{:S(2)}) copy-start(f32[1,512]{1,0:T(1,128)S(1)} %get-tuple-element.280) | copy-start | bytes 6148
  90.6 7.2 copy-start.15
  125.6 6.2 copy-start.63
  125.6 80.3 %all-to-all-start = ((bf16[8,394,512]{2,1,0:T(8,128)(2,1)}), bf16[8,394,512]{2,1,0:T(8,128)(2,1)}, u32[]{:S(2)}, u32[]{:S(2)}) async-start(bf16[8,394,512]{2,1,0:T(8,128)(2,1)} %reshape.253), calls=%async_computation | async-start | bytes 6553600 | tf_op jit(solution)/shard_map/all_to_all | solution.py:115
  230.6 9.4 %copy-start.1 = (f32[788,2048]{1,0:T(8,128)S(1)}, f32[788,2048]{1,0:T(8,128)}, u32[]{:S(2)}) copy-start(f32[788,2048]{1,0:T(8,128)} %get-tuple-element.409) | copy-start | bytes 19365892 | tf_op jit(solution)/shard_map/while
  230.7 9.4 %copy-start.2 = (f32[788,2048]{1,0:T(8,128)S(1)}, f32[788,2048]{1,0:T(8,128)}, u32[]{:S(2)}) copy-start(f32[788,2048]{1,0:T(8,128)} %get-tuple-element.410) | copy-start | bytes 19365892 | tf_op jit(solution)/shard_map/while
  271.1 10.6 %copy-start.1 = (f32[788,2048]{1,0:T(8,128)S(1)}, f32[788,2048]{1,0:T(8,128)}, u32[]{:S(2)}) copy-start(f32[788,2048]{1,0:T(8,128)} %get-tuple-element.409) | copy-start | bytes 19365892 | tf_op jit(solution)/shard_map/while
  271.1 10.6 %copy-start.2 = (f32[788,2048]{1,0:T(8,128)S(1)}, f32[788,2048]{1,0:T(8,128)}, u32[]{:S(2)}) copy-start(f32[788,2048]{1,0:T(8,128)} %get-tuple-element.410) | copy-start | bytes 19365892 | tf_op jit(solution)/shard_map/while
  312.7 10.6 %copy-start.1 = (f32[788,2048]{1,0:T(8,128)S(1)}, f32[788,2048]{1,0:T(8,128)}, u32[]{:S(2)}) copy-start(f32[788,2048]{1,0:T(8,128)} %get-tuple-element.409) | copy-start | bytes 19365892 | tf_op jit(solution)/shard_map/while
  312.7 10.6 %copy-start.2 = (f32[788,2048]{1,0:T(8,128)S(1)}, f32[788,2048]{1,0:T(8,128)}, u32[]{:S(2)}) copy-start(f32[788,2048]{1,0:T(8,128)} %get-tuple-element.410) | copy-start | bytes 19365892 | tf_op jit(solution)/shard_map/while
  354.3 10.6 %copy-start.1 = (f32[788,2048]{1,0:T(8,128)S(1)}, f32[788,2048]{1,0:T(8,128)}, u32[]{:S(2)}) copy-start(f32[788,2048]{1,0:T(8,128)} %get-tuple-element.409) | copy-start | bytes 19365892 | tf_op jit(solution)/shard_map/while
  354.3 10.6 %copy-start.2 = (f32[788,2048]{1,0:T(8,128)S(1)}, f32[788,2048]{1,0:T(8,128)}, u32[]{:S(2)}) copy-start(f32[788,2048]{1,0:T(8,128)} %get-tuple-element.410) | copy-start | bytes 19365892 | tf_op jit(solution)/shard_map/while
  382.5 81.7 %all-to-all-start.3 = ((bf16[8,394,512]{2,1,0:T(8,128)(2,1)}), bf16[8,394,512]{2,1,0:T(8,128)(2,1)}, u32[]{:S(2)}, u32[]{:S(2)}) async-start(bf16[8,394,512]{2,1,0:T(8,128)(2,1)} %reshape.260), calls=%async_computation.3 | async-start | bytes 6553600 | tf_op jit(solution)/shard_map/all_to_all | solution.py:195
  464.2 7.2 copy-start.55
  464.2 7.2 copy-start.38
  464.2 7.2 copy-start.42
  464.2 78.8 %all-to-all-start.1 = ((bf16[8,394,512]{2,1,0:T(8,128)(2,1)}), bf16[8,394,512]{2,1,0:T(8,128)(2,1)}, u32[]{:S(2)}, u32[]{:S(2)}) async-start(bf16[8,394,512]{2,1,0:T(8,128)(2,1)} %reshape.255), calls=%async_computation.1 | async-start | bytes 6553600 | tf_op jit(solution)/shard_map/all_to_all | solution.py:127
  470.2 172.7 %all-reduce.10.cloned.1.call-start = ((), (), s32[]{:S(2)}) async-start(), calls=%async_computation.16 | async-start | bytes 8388608 | tf_op jit(solution)/shard_map/psum | solution.py:190
  477.1 224.3 %reduce-scatter.14.cloned.1.call-start = ((), (), s32[]{:S(2)}) async-start(), calls=%async_computation.11 | async-start | bytes 655360 | tf_op jit(solution)/shard_map/reduce_scatter | solution.py:268
  562.1 19.0 %copy-start.7 = (f32[788,512]{1,0:T(8,128)S(1)}, f32[788,512]{1,0:T(8,128)}, u32[]{:S(2)}) copy-start(f32[788,512]{1,0:T(8,128)} %copy-done.6) | copy-start | bytes 4841476
  562.2 19.0 %copy-start.45 = (f32[788]{0:T(1024)S(1)}, f32[788]{0:T(1024)}, u32[]{:S(2)}) copy-start(f32[788]{0:T(1024)} %copy-done.44) | copy-start | bytes 9460
  562.2 19.0 %copy-start.49 = (f32[788]{0:T(1024)S(1)}, f32[788]{0:T(1024)}, u32[]{:S(2)}) copy-start(f32[788]{0:T(1024)} %copy-done.48) | copy-start | bytes 9460
  562.2 19.0 %copy-start.51 = (f32[1,512]{1,0:T(1,128)S(1)}, f32[1,512]{1,0:T(1,128)}, u32[]{:S(2)}) copy-start(f32[1,512]{1,0:T(1,128)} %copy-done.50) | copy-start | bytes 6148
  589.2 10.4 %slice-start = ((s8[6553600]{0:T(1024)(128)(4,1)}), s8[2359296]{0:T(1024)(128)(4,1)S(1)}, s32[]{:S(2)}) async-start(s8[6553600]{0:T(1024)(128)(4,1)} %bitcast.138), calls=%async_computation.17 | async-start | bytes 4718592
  591.5 8.0 copy-start.18
  591.5 8.0 slice-start.1
  609.2 92.3 %reduce-scatter.12.cloned.1.call-start = ((), (), s32[]{:S(2)}) async-start(), calls=%async_computation.10 | async-start | bytes 1966080 | tf_op jit(solution)/shard_map/reduce_scatter | solution.py:265
  620.4 7.7 copy-start.14
  620.4 7.7 copy-start.57
  620.4 7.7 copy-start.59
  620.4 7.7 copy-start.61
  620.4 7.7 copy-start.66
  631.5 79.9 %reduce-scatter.18.cloned.1.call-start = ((), (), s32[]{:S(2)}) async-start(), calls=%async_computation.13 | async-start | bytes 163840
  654.2 47.2 %copy-start.12 = (f32[788,512]{1,0:T(8,128)S(1)}, f32[788,512]{1,0:T(8,128)}, u32[]{:S(2)}) copy-start(f32[788,512]{1,0:T(8,128)} %copy-done.11) | copy-start | bytes 4841476
  658.8 53.5 %reduce-scatter.16.cloned.1.call-start = ((), (), s32[]{:S(2)}) async-start(), calls=%async_computation.12 | async-start | bytes 163840
  659.8 68.1 %reduce-scatter.20.cloned.1.call-start = ((), (), s32[]{:S(2)}) async-start(), calls=%async_computation.14 | async-start | bytes 163840
  660.7 143.2 %all-reduce.8.cloned.1.call-start = ((), (), s32[]{:S(2)}) async-start(), calls=%async_computation.15 | async-start | bytes 1048576 | tf_op jit(solution)/shard_map/psum | solution.py:282
  (53 other events, 192.8 us)
Sparse Core Ops, SparseCore 0:
  9.6 22.3 all-gather.1
  477.3 87.0 all-reduce.9
  609.3 20.7 reduce-scatter.13
  633.1 28.1 reduce-scatter.11
  663.7 19.5 reduce-scatter.17
  686.1 19.5 reduce-scatter.15
  708.3 19.5 reduce-scatter.19
  731.4 72.5 all-reduce.7
where the time goes:
time: 824 us; the launch traced here: 815 us
  matrix products  271 us (33%)
  waiting for transfers between devices  191 us (23%)
  local copies, waits for them, and re-layouts  129 us (16%)
  blocking collectives  93 us (11%)
  other arithmetic  89.1 us (11%)
  starting transfers between devices  24.7 us (3%)
  between operations  15.5 us (2%)
    dot_general x4, matrix products, one_block(): jnp.dot(active, down_matrix, preferred_element_type=jnp.float32)  74.1 us
    dot_general x4, matrix products, expert_back(): jnp.dot(row_block, up_matrix, preferred_element_type=jnp.float32)  71.5 us
    all_to_all x1, waiting for transfers between devices, local(): lax.all_to_all(send_rows, 'expert', split_axis=0, concat_axis=0, tiled=True)  70.5 us
    all_to_all x1, waiting for transfers between devices, local(): lax.all_to_all(produced, 'expert', split_axis=0, concat_axis=0, tiled=True)  52.5 us
    psum x1, waiting for transfers between devices, local(): lax.psum(owned_in.astype(jnp.bfloat16), 'expert').astype(jnp.float32)  52.1 us
    dot_general x4, matrix products, expert_back(): lax.dot_general(active_low, incoming, contract_rows, preferred_element_ty...  41.2 us
    psum x1, blocking collectives, local(): total_squares = lax.psum(local_squares, ('expert', 'shard'))  38.6 us
    dot_general x4, matrix products, expert_back(): lax.dot_general(incoming, down_matrix, contract_cols, preferred_element_t...  22.6 us
  transfers between devices with their start and end apart: 12, of which 4 were waited for; matrix products, arithmetic and copies ran while one was open for 37% of the time, Pallas kernels for 0%

commit v1 on v0

v1 whole, which is shorter than its diff:
```python
import functools

import jax
import jax.numpy as jnp
from jax import lax
from jax.experimental import pallas as pl
from jax.experimental.pallas import tpu as pltpu
from jax.sharding import PartitionSpec as P

HEAD = 64
SLAB = 2 * HEAD
TOP = 2
EPSILON = 1e-06
F32, BF16 = jnp.float32, jnp.bfloat16
VMEM_LIMIT = 60 * 1024 * 1024


def dot_of(contract):
    def run(left, right):
        return lax.dot_general(
            left, right, (contract, ((), ())), preferred_element_type=F32
        )

    return run


mm = dot_of(((1,), (0,)))
mt = dot_of(((1,), (1,)))
tm = dot_of(((0,), (0,)))


def up_to(value, step):
    return -(-value // step) * step


def normalize(values):
    centre = values - jnp.mean(values, axis=-1, keepdims=True)
    inverse = lax.rsqrt(jnp.mean(centre * centre, axis=-1, keepdims=True) + EPSILON)
    return centre * inverse, inverse


def normalize_back(incoming, unit, inverse, weight):
    scaled = incoming * weight
    first_mean = jnp.mean(scaled, axis=-1, keepdims=True)
    second_mean = jnp.mean(scaled * unit, axis=-1, keepdims=True)
    return inverse * (scaled - first_mean - unit * second_mean)


def gelu_pair(value):
    size = jnp.abs(value)
    t = 1.0 / (1.0 + (0.3275911 * 0.7071067811865476) * size)
    bell = jnp.exp(-0.5 * value * value)
    poly = 0.5 * 1.061405429
    for c in (-1.453152027, 1.421413741, -0.284496736, 0.254829592):
        poly = poly * t + 0.5 * c
    tail = poly * t * bell
    normal = jnp.where(value >= 0, 1.0 - tail, tail)
    return value * normal, normal + value * (bell * 0.3989422804014327)


def call(body, outs, args, scratch=(), cost=None):
    whole = pl.BlockSpec(memory_space=pltpu.VMEM)
    return pl.pallas_call(
        body,
        out_shape=[jax.ShapeDtypeStruct(s, d) for s, d in outs],
        in_specs=[whole] * len(args),
        out_specs=[whole] * len(outs),
        scratch_shapes=list(scratch),
        cost_estimate=cost,
        compiler_params=pltpu.CompilerParams(vmem_limit_bytes=VMEM_LIMIT),
    )(*args)


def place_kernel(col_in, row_in, col_out, row_out):
    tokens = col_in.shape[0]
    down = lax.broadcasted_iota(jnp.int32, (tokens, tokens), 0)
    across = lax.broadcasted_iota(jnp.int32, (tokens, tokens), 1)
    lanes = lax.broadcasted_iota(jnp.int32, col_out.shape, 1)
    named = (col_in[:, 0:1] == lanes) | (col_in[:, 1:2] == lanes)
    before = (across < down).astype(F32).astype(BF16)
    ranks = mm(before, named.astype(F32).astype(BF16))
    col_out[...] = jnp.where(named, ranks, -1.0)
    lines = lax.broadcasted_iota(jnp.int32, row_out.shape, 0)
    named = (row_in[0:1, :] == lines) | (row_in[1:2, :] == lines)
    before = (down < across).astype(F32).astype(BF16)
    ranks = mm(named.astype(F32).astype(BF16), before)
    row_out[...] = jnp.where(named, ranks, -1.0)


def chosen(row_ref, expert, slots):
    tokens = row_ref.shape[1]
    index = lax.broadcasted_iota(jnp.int32, (slots, tokens), 0).astype(F32)
    return jnp.where(index == row_ref[pl.ds(expert, 1), :], 1.0, 0.0).astype(BF16)


def taken(col, expert, slots):
    index = lax.broadcasted_iota(jnp.int32, (col.shape[0], slots), 1).astype(F32)
    return jnp.where(index == col[:, expert : expert + 1], 1.0, 0.0).astype(BF16)


def dispatch_grads_kernel(cot, gates, routes, row, out):
    experts, slots, _ = out.shape
    upstream = cot[...].astype(F32)
    for e in range(experts):
        gate = jnp.where(routes[:, 0:1] == e, gates[:, 0:1], 0.0) + jnp.where(
            routes[:, 1:2] == e, gates[:, 1:2], 0.0
        )
        scaled = (upstream * gate).astype(BF16)
        out[e] = mm(chosen(row, e, slots), scaled).astype(BF16)


def forward_kernel(
    images, real, x, w_in, w_out, gain, shift, bias, row, middle_out, qkv, context, send, squares, ctx_t
):
    tokens, width = x.shape
    lines = tokens // images
    stream = x[...].astype(F32)
    unit, _ = normalize(stream)
    normed = (unit * gain[0:1, :] + shift[0:1, :]).astype(BF16)
    projected = mm(normed, w_in[...])
    qkv[:, :width] = (projected[:, :width] + bias[0:1, :]).astype(BF16)
    qkv[:, width : 2 * width] = projected[:, width : 2 * width].astype(BF16)
    qkv[:, 2 * width :] = (projected[:, 2 * width :] + bias[1:2, :]).astype(BF16)
    valid = lax.broadcasted_iota(jnp.int32, (lines, lines), 0) < real
    half = lax.broadcasted_iota(jnp.int32, (lines, SLAB), 1) < HEAD

    def one_image(i, carry):
        rows = pl.ds(pl.multiple_of(i * lines, 16), lines)
        for s in range(width // SLAB):
            q = qkv[rows, s * SLAB : (s + 1) * SLAB]
            k = qkv[rows, width + s * SLAB : width + (s + 1) * SLAB]
            v = qkv[rows, 2 * width + s * SLAB : 2 * width + (s + 1) * SLAB]
            parts = []
            for h in range(2):
                keep = half if h == 0 else ~half
                scores = mt(jnp.where(keep, k, jnp.zeros_like(k)), q) * (HEAD**-0.5)
                scores = jnp.where(valid, scores, -1e30)
                powers = jnp.exp(scores - jnp.max(scores, axis=0, keepdims=True))
                soft = powers / jnp.sum(powers, axis=0, keepdims=True)
                parts.append(tm(soft.astype(BF16), v))
            context[rows, s * SLAB : (s + 1) * SLAB] = jnp.where(half, parts[0], parts[1]).astype(BF16)
        return carry

    lax.fori_loop(0, images, one_image, 0)
    middle = stream + mm(context[...], w_out[...]) + bias[2:3, :]
    middle_out[...] = middle
    unit, _ = normalize(middle)
    normed = (unit * gain[1:2, :] + shift[1:2, :]).astype(BF16)
    experts, slots, _ = send.shape
    for e in range(experts):
        send[e] = mm(chosen(row, e, slots), normed).astype(BF16)
    index = lax.broadcasted_iota(jnp.int32, (tokens, 1), 0)
    counts = jnp.where(lax.rem(index, lines) < real, 1.0, 0.0)
    squares[0:1, :] = jnp.sum(stream * stream, axis=0, keepdims=True)
    squares[1:2, :] = jnp.sum(middle * middle * counts, axis=0, keepdims=True)


def expert_kernel(
    chunk, rows, grads, up, hidden_bias, down, out_bias, made, back, d_up, d_hidden, d_down, d_out, sum_up, sum_down
):
    step, steps = pl.program_id(0), pl.num_programs(0)

    @pl.when(step == 0)
    def _():
        sum_up[...] = jnp.zeros_like(sum_up)
        sum_down[...] = jnp.zeros_like(sum_down)
        d_hidden[...] = jnp.zeros_like(d_hidden)
        d_out[...] = jnp.zeros_like(d_out)

    x, g = rows[...], grads[...]
    produced = jnp.zeros(x.shape, F32)
    routed = jnp.zeros(x.shape, F32)
    for j in range(up.shape[1] // chunk):
        cols = slice(j * chunk, (j + 1) * chunk)
        hidden = mm(x, up[:, cols]) + hidden_bias[:, cols]
        back_active = mt(g, down[cols, :])
        active, slope = gelu_pair(hidden)
        active = active.astype(BF16)
        back_hidden = back_active * slope
        d_hidden[:, cols] += jnp.sum(back_hidden, axis=0, keepdims=True)
        back_hidden = back_hidden.astype(BF16)
        produced += mm(active, down[cols, :])
        routed += mt(back_hidden, up[:, cols])
        sum_up[:, cols] += tm(x, back_hidden)
        sum_down[:, cols] += tm(g, active)
    d_out[...] += jnp.sum(g.astype(F32), axis=0, keepdims=True)
    made[...] = (produced + out_bias[...]).astype(BF16)
    back[...] = routed.astype(BF16)

    @pl.when(step == steps - 1)
    def _():
        d_up[...] = sum_up[...].astype(BF16)
        d_down[...] = sum_down[...].T.astype(BF16)


def backward_kernel(
    images, real, x, w_in, w_out, gain, shift, qkv, context, middle, cot, col, back,
    d_x, d_in, d_out, d_gain, d_shift, d_bias, d_qkv, d_context,
):
    tokens, width = x.shape
    lines = tokens // images
    experts, slots, _ = back.shape
    back_two = jnp.zeros((tokens, width), F32)
    for e in range(experts):
        back_two += mm(taken(col, e, slots), back[e])
    unit, inverse = normalize(middle[...])
    d_gain[1:2, :] = jnp.sum(back_two * unit, axis=0, keepdims=True)
    d_shift[1:2, :] = jnp.sum(back_two, axis=0, keepdims=True)
    back_middle = cot[...].astype(F32) + normalize_back(back_two, unit, inverse, gain[1:2, :])
    d_x[...] = back_middle
    branch = back_middle.astype(BF16)
    d_bias[2:3, :] = jnp.sum(branch.astype(F32), axis=0, keepdims=True)
    d_out[...] = tm(context[...], branch).astype(BF16)
    d_context[...] = mt(branch, w_out[...]).astype(BF16)
    valid = lax.broadcasted_iota(jnp.int32, (lines, lines), 0) < real
    half = lax.broadcasted_iota(jnp.int32, (lines, SLAB), 1) < HEAD
    scale = HEAD**-0.5
    d_bias[0:2, :] = jnp.zeros((2, width), F32)

    def one_image(i, carry):
        rows = pl.ds(pl.multiple_of(i * lines, 16), lines)
        for s in range(width // SLAB):
            cols = [slice(a * width + s * SLAB, a * width + (s + 1) * SLAB) for a in range(3)]
            q, k, v = (qkv[rows, c] for c in cols)
            given = d_context[rows, cols[0]]
            parts = []
            for h in range(2):
                keep = half if h == 0 else ~half
                zero = jnp.zeros_like(k)
                scores = mt(jnp.where(keep, k, zero), q) * scale
                scores = jnp.where(valid, scores, -1e30)
                powers = jnp.exp(scores - jnp.max(scores, axis=0, keepdims=True))
                soft = powers / jnp.sum(powers, axis=0, keepdims=True)
                back_soft = mt(jnp.where(keep, v, zero), given)
                shared = jnp.sum(back_soft * soft, axis=0, keepdims=True)
                back_scores = (soft * (back_soft - shared)).astype(BF16)
                parts.append((tm(back_scores, k), mm(back_scores, q), mm(soft.astype(BF16), given)))
            grads = [jnp.where(half, a, b) for a, b in zip(*parts)]
            grads = [grads[0] * scale, grads[1] * scale, grads[2]]
            d_bias[0:1, cols[0]] += jnp.sum(grads[0], axis=0, keepdims=True)
            d_bias[1:2, cols[0]] += jnp.sum(grads[2], axis=0, keepdims=True)
            for c, grad in zip(cols, grads):
                d_qkv[rows, c] = grad.astype(BF16)
        return carry

    lax.fori_loop(0, images, one_image, 0)
    unit, inverse = normalize(x[...].astype(F32))
    normed = (unit * gain[0:1, :] + shift[0:1, :]).astype(BF16)
    d_in[...] = tm(normed, d_qkv[...]).astype(BF16)
    back_one = mt(d_qkv[...], w_in[...])
    d_gain[0:1, :] = jnp.sum(back_one * unit, axis=0, keepdims=True)
    d_shift[0:1, :] = jnp.sum(back_one, axis=0, keepdims=True)
    d_x[...] += normalize_back(back_one, unit, inverse, gain[0:1, :])


def output_kernel(lines, real, middle, cot, gates, routes, col, returned, out, d_gates, squares):
    tokens, width = middle.shape
    experts, slots, _ = returned.shape
    rows = [jnp.zeros((tokens, width), F32) for _ in range(TOP)]
    for r in range(TOP):
        for e in range(experts):
            mine = jnp.where(routes[:, r : r + 1] == e, col[:, e : e + 1], -1.0)
            rows[r] += mm(taken(mine, 0, slots), returned[e])
    upstream = cot[...].astype(F32)
    total = middle[...]
    for r in range(TOP):
        total += rows[r] * gates[:, r : r + 1]
        d_gates[:, r : r + 1] = jnp.sum(rows[r] * upstream, axis=1, keepdims=True)
    out[...] = total.astype(BF16)
    index = lax.broadcasted_iota(jnp.int32, (tokens, 1), 0)
    counts = jnp.where(lax.rem(index, lines) < real, 1.0, 0.0)
    squares[...] = jnp.sum(total * total * counts, axis=0, keepdims=True)


def local(
    images, attention_in, attention_out, layer_gain, layer_shift, attention_bias, expert_up, hidden_bias,
    expert_down, expert_bias, routes, gates, cotangent,
):
    count, real, width = images.shape
    lines = up_to(real, 16)
    tokens = count * lines
    experts = lax.axis_size("expert")
    shards = lax.axis_size("shard")
    slots = up_to(max(2, 4 * count * real // experts), 16)
    hidden_units = expert_up.shape[2]

    def padded(values, fill=0):
        wide = jnp.pad(values, ((0, 0), (0, lines - real), (0, 0)), constant_values=fill)
        return wide.reshape(tokens, values.shape[2])

    matrices = jnp.concatenate([attention_in, attention_out], axis=1)
    vectors = jnp.concatenate([layer_gain, layer_shift, attention_bias], axis=0)
    matrices = lax.all_gather(matrices, "shard", axis=0, tiled=True)
    vectors = lax.all_gather(vectors, "shard", axis=1, tiled=True).astype(F32)
    full_in, full_out = matrices[:, : 3 * width], matrices[:, 3 * width :]
    gain, shift, bias = vectors[0:2], vectors[2:4], vectors[4:7]

    x, cot = padded(images), padded(cotangent)
    route_col, gate_col = padded(routes, -1), padded(gates)
    col, row = call(
        place_kernel,
        [((tokens, up_to(experts, 128)), F32), ((up_to(experts, 8), tokens), F32)],
        [route_col, route_col.T],
    )
    block = (experts, slots, width)
    send_grads = call(dispatch_grads_kernel, [(block, BF16)], [cot, gate_col, route_col, row])[0]
    exchange = functools.partial(
        lax.all_to_all, axis_name="expert", split_axis=0, concat_axis=0, tiled=True
    )
    grads = exchange(send_grads)
    middle, qkv, context, send_rows, squares = call(
        functools.partial(forward_kernel, count, real),
        [
            ((tokens, width), F32), ((tokens, 3 * width), BF16), ((tokens, width), BF16), (block, BF16),
            ((2, width), F32),
        ],
        [x, full_in, full_out, gain, shift, bias, row],
        [pltpu.VMEM((8, 128), F32)],
    )
    rows = exchange(send_rows)

    every = experts * slots
    steps = 8
    size = every // steps
    tile = lambda: pl.BlockSpec((size, width), lambda i: (i, 0))
    fixed = lambda *shape: pl.BlockSpec(shape, lambda i: (0, 0))
    made, back, d_up, d_hidden, d_down, d_eb = pl.pallas_call(
        functools.partial(expert_kernel, 512),
        grid=(steps,),
        out_shape=[
            jax.ShapeDtypeStruct((every, width), BF16),
            jax.ShapeDtypeStruct((every, width), BF16),
            jax.ShapeDtypeStruct((width, hidden_units), BF16),
            jax.ShapeDtypeStruct((1, hidden_units), F32),
            jax.ShapeDtypeStruct((hidden_units, width), BF16),
            jax.ShapeDtypeStruct((1, width), F32),
        ],
        in_specs=[
            tile(), tile(), fixed(width, hidden_units), fixed(1, hidden_units), fixed(hidden_units, width),
            fixed(1, width),
        ],
        out_specs=[
            tile(), tile(), fixed(width, hidden_units), fixed(1, hidden_units), fixed(hidden_units, width),
            fixed(1, width),
        ],
        scratch_shapes=[pltpu.VMEM((width, hidden_units), F32), pltpu.VMEM((width, hidden_units), F32)],
        compiler_params=pltpu.CompilerParams(vmem_limit_bytes=VMEM_LIMIT),
    )(
        rows.reshape(every, width), grads.reshape(every, width), expert_up[0], hidden_bias.astype(F32),
        expert_down[0], expert_bias.astype(F32),
    )
    routed = exchange(back.reshape(block))
    returned = exchange(made.reshape(block))
    up_total = lax.psum(d_up, "shard").astype(F32)
    down_total = lax.psum(d_down, "shard").astype(F32)
    small = jnp.concatenate([d_hidden, d_eb], axis=1).astype(BF16)
    small = lax.psum(small, "shard").astype(F32)

    d_x, d_in, d_out, d_gain, d_shift, d_bias = call(
        functools.partial(backward_kernel, count, real),
        [
            ((tokens, width), F32), ((width, 3 * width), BF16), ((width, width), BF16), ((2, width), F32),
            ((2, width), F32), ((3, width), F32),
        ],
        [x, full_in, full_out, gain, shift, qkv, context, middle, cot, col, routed],
        [pltpu.VMEM((tokens, 3 * width), BF16), pltpu.VMEM((tokens, width), BF16)],
    )
    block_output, d_gates, last = call(
        functools.partial(output_kernel, lines, real),
        [((tokens, width), BF16), ((tokens, TOP), F32), ((1, width), F32)],
        [middle, cot, gate_col, route_col, col, returned],
    )
    sums = jnp.sum(jnp.concatenate([squares, last], axis=0), axis=1)
    sums = lax.psum(sums, ("expert", "shard"))
    magnitude = jnp.sqrt(sums / float(count * real * width * experts * shards))

    seven = jnp.concatenate([d_gain, d_shift, d_bias], axis=0).astype(BF16)
    seven = jnp.pad(seven, ((0, 1), (0, 0))).T
    owned = jnp.concatenate([d_in, d_out, jnp.pad(seven, ((0, 0), (0, 120)))], axis=1)
    owned = lax.psum_scatter(owned, "shard", scatter_dimension=0, tiled=True)
    owned = lax.psum(owned, "expert").astype(F32)
    vectors = owned[:, 4 * width : 4 * width + 8].T

    def cut(values):
        return values.reshape(count, lines, values.shape[1])[:, :real]

    return (
        cut(block_output),
        cut(d_x),
        owned[:, : 3 * width],
        owned[:, 3 * width : 4 * width],
        vectors[0:2],
        vectors[2:4],
        vectors[4:7],
        up_total[None],
        small[:, :hidden_units],
        down_total[None],
        small[:, hidden_units:],
        cut(d_gates),
        magnitude,
    )


def solution(mesh):
    every = P(("expert", "shard"), None, None)
    return jax.shard_map(
        local,
        mesh=mesh,
        in_specs=(
            every, P("shard", None), P("shard", None), P(None, "shard"), P(None, "shard"), P(None, "shard"),
            P("expert", None, None), P("expert", None), P("expert", None, None), P("expert", None),
            every, every, every,
        ),
        out_specs=(
            every, every, P("shard", None), P("shard", None), P(None, "shard"), P(None, "shard"),
            P(None, "shard"), P("expert", None, None), P("expert", None), P("expert", None, None),
            P("expert", None), every, P(),
        ),
        check_vma=False,
    )
```

time: 824 us -> 574 us (0.70)
  matrix products: 271 us -> 0 us
  Pallas kernels: 0 us -> 134 us
  local copies, waits for them, and re-layouts: 129 us -> 25.7 us
  other arithmetic: 89.1 us -> 19.3 us
  blocking collectives: 93 us -> 134 us
  waiting for transfers between devices: 191 us -> 225 us
  starting transfers between devices: 24.7 us -> 15.9 us
    dot_general x36 -> x0, matrix products: 271 us -> none  [the longest x4 74.1 us: one_block(): jnp.dot(active, down_matrix, preferred_element_type=jnp.float32)]
    pallas_call x0 -> x6, Pallas kernels: none -> 134 us  [the longest x1 69.1 us: local(): pl.pallas_call(functools.partial(expert_kernel, 512), grid=(steps,), out_...]
    all_to_all x0 -> x1, blocking collectives: none -> 78.2 us  [local(): routed = exchange(back.reshape(block))]
    reshape x21 -> x0, local copies, waits for them, and re-layouts: 47.9 us -> none  [the longest x2 5.38 us: local(): projected[:, model_width:2 * model_width].astype(jnp.bfloat16)]
    reduce_sum x15 -> x1, other arithmetic: 36.5 us -> 0.8 us  [local(): sums = jnp.sum(jnp.concatenate([squares, last], axis=0), axis=1)]
    psum x2, waiting for transfers between devices: 52.1 us -> 84.4 us  [the longest x1 76.1 us: local(): up_total = lax.psum(d_up, 'shard').astype(F32)]
    reduce_scatter x2 -> x1, waiting for transfers between devices: 0.01 us -> 26.3 us  [local(): owned = lax.psum_scatter(owned, 'shard', scatter_dimension=0, tiled=True)]
    all_to_all x4 -> x3, waiting for transfers between devices: 123 us -> 98.2 us  [the longest x1 71.6 us: local(): rows = exchange(send_rows)]
  transfers between devices with their start and end apart: 12 -> 7, of which waited for: 4 -> 6; matrix products, arithmetic and copies ran while one was open for 37% -> 5% of each run, Pallas kernels for 0% -> 5%
where the time goes in v1:
time: 574 us; the launch traced here: 569 us
  waiting for transfers between devices  225 us (39%)
  Pallas kernels  134 us (23%)
  blocking collectives  134 us (23%)
  local copies, waits for them, and re-layouts  25.7 us (4%)
  other arithmetic  19.3 us (3%)
  starting transfers between devices  15.9 us (3%)
  between operations  14.3 us (2%)
    all_to_all x1, blocking collectives, local(): routed = exchange(back.reshape(block))  78.2 us
    psum x1, waiting for transfers between devices, local(): up_total = lax.psum(d_up, 'shard').astype(F32)  76.1 us
    all_to_all x1, waiting for transfers between devices, local(): rows = exchange(send_rows)  71.6 us
    pallas_call x1, Pallas kernels, local(): pl.pallas_call(functools.partial(expert_kernel, 512), grid=(steps,), out_...  69.1 us
    pallas_call x5, Pallas kernels, call(): pl.pallas_call(body, out_shape=[jax.ShapeDtypeStruct(s, d) for s, d in ou...  65.2 us
    psum x1, blocking collectives, local(): sums = lax.psum(sums, ('expert', 'shard'))  39.5 us
    all_to_all x1, waiting for transfers between devices, local(): grads = exchange(send_grads)  26.7 us
    reduce_scatter x1, waiting for transfers between devices, local(): owned = lax.psum_scatter(owned, 'shard', scatter_dimension=0, tiled=True)  26.3 us
  transfers between devices with their start and end apart: 7, of which 6 were waited for; matrix products, arithmetic and copies ran while one was open for 5% of the time, Pallas kernels for 5%

profile of v1, /device:TPU:0, one launch (start us, length us, event | category | flops | bytes accessed | tf_op | source)
XLA Modules:
  0.0 569.2 jit_solution(8337894987697504601)
XLA Ops:
  7.2 1.0 copy.42
  8.2 0.8 copy.28.row_in
  9.0 0.9 copy.44
  10.0 0.8 pad.26.clone
  10.8 2.6 shard_map.228
  13.4 1.0 pad.25.clone
  14.4 6.9 %shard_map.230 = bf16[8,400,512]{2,1,0:T(8,128)(2,1)} custom-call(bf16[832,512]{1,0:T(8,128)(2,1)} %bitcast.21, f32[832,2]{1,0:T(8,128)} %bitcast.31, s32[832,2]{1,0:T(8,128)} %bitcast.27, f32[8,832]{1,0:T(8,128)} %get-tuple-element.35.row), custom_call_target="tpu_custom_call" | custom-call | tf_op jit(solution)/shard_map/pallas_call | solution.py:63
  21.3 7.4 %all-to-all-start.1 = ((bf16[8,400,512]{2,1,0:T(8,128)(2,1)}), bf16[8,400,512]{2,1,0:T(8,128)(2,1)S(1)}, u32[]{:S(2)}, u32[]{:S(2)}) async-start(bf16[8,400,512]{2,1,0:T(8,128)(2,1)} %shard_map.230), calls=%async_computation.1 | async-start | bytes 6553600 | tf_op jit(solution)/shard_map/all_to_all | solution.py:310
  28.8 1.8 pad_maximum_fusion
  30.7 5.7 all_gather.7
  37.0 1.3 copy.41
  38.3 1.0 pad.23.clone
  39.9 15.8 %all-gather.2.cloned.1.call-done = bf16[512,2048]{1,0:T(8,128)(2,1)} async-done(((bf16[128,2048]{1,0:T(8,128)(2,1)}), bf16[512,2048]{1,0:T(8,128)(2,1)}) %all-gather.2.cloned.1.call-update) | async-done | bytes 2097168 | tf_op jit(solution)/shard_map/all_gather | solution.py:293
  55.7 1.9 slice.65.w_out
  57.6 2.7 slice.64.w_in
  60.2 15.4 %shard_map.229 = (f32[832,512]{1,0:T(8,128)}, bf16[832,1536]{1,0:T(8,128)(2,1)}, bf16[832,512]{1,0:T(8,128)(2,1)}, bf16[8,400,512]{2,1,0:T(8,128)(2,1)}, f32[2,512]{1,0:T(2,128)}) custom-call(bf16[832,512]{1,0:T(8,128)(2,1)} %bitcast.29, bf16[512,1536]{1,0:T(8,128)(2,1)} %slice.64.w_in, bf16[512,512]{1,0:T(8,128)(2,1)} %slice.65.w_out, ...), custom_call_target="tpu_custom_call" | custom-call | tf_op jit(solution)/shard_map/pallas_call | solution.py:63
  75.6 26.7 %all-to-all-done.1 = bf16[8,400,512]{2,1,0:T(8,128)(2,1)S(1)} async-done(((bf16[8,400,512]{2,1,0:T(8,128)(2,1)}), bf16[8,400,512]{2,1,0:T(8,128)(2,1)S(1)}, u32[]{:S(2)}, u32[]{:S(2)}) %all-to-all-start.1) | async-done | bytes 3276832 | tf_op jit(solution)/shard_map/all_to_all | solution.py:310
  102.3 1.7 copy-done.1
  104.0 4.5 all-to-all-start
  109.8 71.6 %all-to-all-done = bf16[8,400,512]{2,1,0:T(8,128)(2,1)} async-done(((bf16[8,400,512]{2,1,0:T(8,128)(2,1)}), bf16[8,400,512]{2,1,0:T(8,128)(2,1)}, u32[]{:S(2)}, u32[]{:S(2)}) %all-to-all-start) | async-done | bytes 3276832 | tf_op jit(solution)/shard_map/all_to_all | solution.py:320
  181.4 69.1 %shard_map.231 = (bf16[3200,512]{1,0:T(8,128)(2,1)}, bf16[3200,512]{1,0:T(8,128)(2,1)}, bf16[512,2048]{1,0:T(8,128)(2,1)}, f32[1,2048]{1,0:T(1,128)}, bf16[2048,512]{1,0:T(8,128)(2,1)}, /*index=5*/f32[1,512]{1,0:T(1,128)}) custom-call(bf16[3200,512]{1,0:T(8,128)(2,1)} %bitcast.5.rows, bf16[3200,512]{1,0:T(8,128)(2,1)} %bitcast.24, ...), custom_call_target="tpu_custom_call" | custom-call | tf_op jit(solution)/shard_map/pallas_call | solution.py:327
  250.5 78.2 %all_to_all.20.back = bf16[8,400,512]{2,1,0:T(8,128)(2,1)} all-to-all(bf16[8,400,512]{2,1,0:T(8,128)(2,1)} %bitcast.34), channel_id=1, replica_groups=mesh['expert'=8,'shard'=4] {'expert'}, dimensions={0} | all-to-all | bytes 6553600 | tf_op jit(solution)/shard_map/all_to_all | solution.py:352
  328.7 28.2 %shard_map.233 = (f32[832,512]{1,0:T(8,128)}, bf16[512,1536]{1,0:T(8,128)(2,1)}, bf16[512,512]{1,0:T(8,128)(2,1)}, f32[2,512]{1,0:T(2,128)}, f32[2,512]{1,0:T(2,128)}, /*index=5*/f32[3,512]{1,0:T(4,128)}) custom-call(bf16[832,512]{1,0:T(8,128)(2,1)} %bitcast.30, bf16[512,1536]{1,0:T(8,128)(2,1)} %slice.64.w_in, bf16[512,512]{1,0:T(8,128)(2,1)} %slice.65.w_out, ...), custom_call_target="tpu_custom_call" | custom-call | tf_op jit(solution)/shard_map/pallas_call | solution.py:63
  356.9 0.7 convert.17
  357.6 0.7 convert.18
  358.3 0.7 convert.19
  359.2 3.1 fusion.1
  362.3 3.7 all-to-all-start.2
  366.1 0.7 all-reduce.12.cloned.1.call-update
  366.8 26.3 %reduce-scatter.2.cloned.1.call-done = bf16[128,2176]{1,0:T(8,128)(2,1)} async-done(((bf16[512,2176]{1,0:T(8,128)(2,1)}), bf16[128,2176]{1,0:T(8,128)(2,1)}) %reduce-scatter.2.cloned.1.call-update) | async-done | bytes 557072 | tf_op jit(solution)/shard_map/reduce_scatter | solution.py:380
  393.2 11.0 %psum.37 = bf16[1,2560]{1,0:T(2,128)(2,1)S(1)} all-reduce(bf16[1,2560]{1,0:T(2,128)(2,1)S(1)} %pad_maximum_fusion.1), channel_id=1, replica_groups=mesh['expert'=8,'shard'=4] {'shard'}, use_global_device_ids=true, to_apply=%region_3.4 | all-reduce | flops 2560 | bytes 10240 | tf_op jit(solution)/shard_map/psum | solution.py:357
  405.3 76.1 %all-reduce.12.cloned.1.call-done = (bf16[1,512,2048]{2,1,0:T(8,128)(2,1)}, bf16[1,2048,512]{2,1,0:T(8,128)(2,1)}) async-done(((bf16[1,512,2048]{2,1,0:T(8,128)(2,1)}, bf16[1,2048,512]{2,1,0:T(8,128)(2,1)}), (bf16[1,512,2048]{2,1,0:T(8,128)(2,1)}, bf16[1,2048,512]{2,1,0:T(8,128)(2,1)})) %all-reduce.12.cloned.1.call-update) | async-done | bytes 4194320 | tf_op jit(solution)/shard_map/psum | solution.py:354
  481.5 4.1 broadcast_in_dim.13
  485.6 1.7 copy-done
  487.3 12.2 %shard_map.232 = (bf16[832,512]{1,0:T(8,128)(2,1)}, f32[832,2]{1,0:T(8,128)}, f32[1,512]{1,0:T(1,128)}) custom-call(f32[832,512]{1,0:T(8,128)} %get-tuple-element.36.middle, bf16[832,512]{1,0:T(8,128)(2,1)} %bitcast.23, f32[832,2]{1,0:T(8,128)} %bitcast.32, s32[832,2]{1,0:T(8,128)} %bitcast.28, f32[832,128]{1,0:T(8,128)} %get-tuple-element.37.col, ...), custom_call_target="tpu_custom_call" | custom-call | tf_op jit(solution)/shard_map/pallas_call | solution.py:63
  499.5 0.8 maximum_reduce_fusion
  500.3 4.3 broadcast_in_dim.15
  504.6 39.5 %psum.39 = f32[3]{0:T(128)S(1)} all-reduce(f32[3]{0:T(128)S(1)} %maximum_reduce_fusion), channel_id=1, replica_groups=mesh['expert'=8,'shard'=4] {'expert','shard'}, use_global_device_ids=true, to_apply=%region_6.7 | all-reduce | flops 3 | bytes 24 | tf_op jit(solution)/shard_map/psum | solution.py:374
  544.2 2.2 copy.39
  546.5 1.3 copy.38
  547.8 0.8 copy.40
  549.1 8.3 %all-reduce.10.cloned.1.call-done = bf16[128,2176]{1,0:T(8,128)(2,1)} async-done(((bf16[128,2176]{1,0:T(8,128)(2,1)}), bf16[128,2176]{1,0:T(8,128)(2,1)}) %all-reduce.10.cloned.1.call-update) | async-done | bytes 557072 | tf_op jit(solution)/shard_map/psum | solution.py:381
  557.4 1.2 convert_element_type.39
  558.8 0.7 copy.37
  559.4 0.6 copy.36
  560.1 0.6 copy.35
  560.7 0.7 slice.72
  561.5 1.0 slice.71
  (61 shorter events, 5.3 us)
Async XLA Ops:
  7.2 2.7 copy-start.5
  8.2 2.6 copy-start.2
  21.3 7.5 %copy-start.8 = (bf16[128,512]{1,0:T(8,128)(2,1)S(1)}, bf16[128,512]{1,0:T(8,128)(2,1)}, u32[]{:S(2)}) copy-start(bf16[128,512]{1,0:T(8,128)(2,1)} %param.15) | copy-start | bytes 393220
  21.3 9.4 %copy-start.14 = (bf16[3,128]{1,0:T(4,128)(2,1)S(1)}, bf16[3,128]{1,0:T(4,128)(2,1)}, u32[]{:S(2)}) copy-start(bf16[3,128]{1,0:T(4,128)(2,1)} %param.18) | copy-start | bytes 2308
  21.3 9.4 %copy-start.15 = (bf16[2,128]{1,0:T(2,128)(2,1)S(1)}, bf16[2,128]{1,0:T(2,128)(2,1)}, u32[]{:S(2)}) copy-start(bf16[2,128]{1,0:T(2,128)(2,1)} %param.17) | copy-start | bytes 1540
  21.3 9.4 %copy-start.16 = (bf16[2,128]{1,0:T(2,128)(2,1)S(1)}, bf16[2,128]{1,0:T(2,128)(2,1)}, u32[]{:S(2)}) copy-start(bf16[2,128]{1,0:T(2,128)(2,1)} %param.16) | copy-start | bytes 1540
  21.3 80.9 %all-to-all-start.1 = ((bf16[8,400,512]{2,1,0:T(8,128)(2,1)}), bf16[8,400,512]{2,1,0:T(8,128)(2,1)S(1)}, u32[]{:S(2)}, u32[]{:S(2)}) async-start(bf16[8,400,512]{2,1,0:T(8,128)(2,1)} %shard_map.230), calls=%async_computation.1 | async-start | bytes 6553600 | tf_op jit(solution)/shard_map/all_to_all | solution.py:310
  28.7 27.0 %all-gather.2.cloned.1.call-start = ((), (), s32[]{:S(2)}) async-start(), calls=%async_computation.5 | async-start | bytes 2621440 | tf_op jit(solution)/shard_map/all_gather | solution.py:293
  102.2 1.7 copy-start.1
  102.2 6.4 %copy-start.12 = (bf16[1,512]{1,0:T(2,128)(2,1)S(1)}, bf16[1,512]{1,0:T(2,128)(2,1)}, u32[]{:S(2)}) copy-start(bf16[1,512]{1,0:T(2,128)(2,1)} %param.22) | copy-start | bytes 3076
  102.2 7.0 %copy-start.9 = (bf16[1,2048]{1,0:T(2,128)(2,1)S(1)}, bf16[1,2048]{1,0:T(2,128)(2,1)}, u32[]{:S(2)}) copy-start(bf16[1,2048]{1,0:T(2,128)(2,1)} %param.20) | copy-start | bytes 12292
  104.0 77.5 %all-to-all-start = ((bf16[8,400,512]{2,1,0:T(8,128)(2,1)}), bf16[8,400,512]{2,1,0:T(8,128)(2,1)}, u32[]{:S(2)}, u32[]{:S(2)}) async-start(bf16[8,400,512]{2,1,0:T(8,128)(2,1)} %get-tuple-element.38), calls=%async_computation | async-start | bytes 6553600 | tf_op jit(solution)/shard_map/all_to_all | solution.py:320
  108.4 284.7 %reduce-scatter.2.cloned.1.call-start = ((), (), s32[]{:S(2)}) async-start(), calls=%async_computation.6 | async-start | bytes 2785280 | tf_op jit(solution)/shard_map/reduce_scatter | solution.py:380
  362.3 123.3 %all-to-all-start.2 = ((bf16[8,400,512]{2,1,0:T(8,128)(2,1)}), bf16[8,400,512]{2,1,0:T(8,128)(2,1)S(1)}, u32[]{:S(2)}, u32[]{:S(2)}) async-start(bf16[8,400,512]{2,1,0:T(8,128)(2,1)} %bitcast.33), calls=%async_computation.2 | async-start | bytes 6553600 | tf_op jit(solution)/shard_map/all_to_all | solution.py:353
  366.0 0.8 copy-start.13
  366.0 0.8 copy-start.10
  366.0 115.5 %all-reduce.12.cloned.1.call-start = ((), (), s32[]{:S(2)}) async-start(), calls=%async_computation.8 | async-start | bytes 8388608 | tf_op jit(solution)/shard_map/psum | solution.py:354
  366.7 190.7 %all-reduce.10.cloned.1.call-start = ((), (), s32[]{:S(2)}) async-start(), calls=%async_computation.7 | async-start | bytes 1114112 | tf_op jit(solution)/shard_map/psum | solution.py:381
  485.6 13.9 %copy-start.11 = (f32[2,512]{1,0:T(2,128)S(1)}, f32[2,512]{1,0:T(2,128)}, u32[]{:S(2)}) copy-start(f32[2,512]{1,0:T(2,128)} %get-tuple-element.55) | copy-start | bytes 12292
  485.6 1.7 copy-start
  500.3 43.8 %copy-start.4 = (f32[832,512]{1,0:T(8,128)S(1)}, f32[832,512]{1,0:T(8,128)}, u32[]{:S(2)}) copy-start(f32[832,512]{1,0:T(8,128)} %get-tuple-element.44) | copy-start | bytes 5111812
  544.2 2.2 copy-start.6
  546.4 1.4 copy-start.7
  557.4 3.3 copy-start.3
Sparse Core Ops, SparseCore 0:
  31.7 23.9 all-gather.1
  362.4 30.6 reduce-scatter.1
  395.7 85.7 all-reduce.11
  484.7 72.6 all-reduce.9

commit v2 on v1

--- a/solution.py
+++ b/solution.py
@@ -58,39 +58,104 @@
     return value * normal, normal + value * (bell * 0.3989422804014327)
 
 
-def call(body, outs, args, scratch=(), cost=None):
-    whole = pl.BlockSpec(memory_space=pltpu.VMEM)
+def call(body, outs, args, scratch=(), outside=(), collective=None):
+    where = [
+        pl.BlockSpec(memory_space=pl.ANY if i in outside else pltpu.VMEM) for i in range(len(args) + len(outs))
+    ]
     return pl.pallas_call(
         body,
         out_shape=[jax.ShapeDtypeStruct(s, d) for s, d in outs],
-        in_specs=[whole] * len(args),
-        out_specs=[whole] * len(outs),
+        in_specs=where[: len(args)],
+        out_specs=where[len(args) :],
         scratch_shapes=list(scratch),
-        cost_estimate=cost,
-        compiler_params=pltpu.CompilerParams(vmem_limit_bytes=VMEM_LIMIT),
+        compiler_params=pltpu.CompilerParams(
+            vmem_limit_bytes=VMEM_LIMIT, collective_id=collective, has_side_effects=collective is not None
+        ),
     )(*args)
 
 
-def place_kernel(col_in, row_in, col_out, row_out):
+def axes():
+    return (
+        lax.axis_index("expert"), lax.axis_index("shard"), lax.axis_size("expert"), lax.axis_size("shard")
+    )
+
+
+def home(shard, shards):
+    core = shard % 2
+    return (shard // 2) * (1 - core) + (shards - 1 - shard // 2) * core
+
+
+def expert_of(member, experts, shards):
+    return home(member % shards, shards) * (experts // shards) + member // shards
+
+
+class Place:
+    def __init__(self):
+        self.expert, self.shard, self.experts, self.shards = axes()
+        self.width = self.experts // self.shards
+        self.row = lax.div(self.expert, self.width)
+        self.member = lax.rem(self.expert, self.width) * self.shards + self.shard
+        self.core = lax.rem(self.shard, 2)
+        self.chip = lax.div(self.shard, 2)
+        self.root = self.chip * (1 - self.core) + (self.shards - 1 - self.chip) * self.core
+
+    def peer(self, step):
+        other = lax.rem(self.member + step, self.experts)
+        return other, (self.row * self.width + lax.div(other, self.shards), lax.rem(other, self.shards))
+
+    def along(self, step):
+        return (self.expert + step * self.width, self.shard)
+
+    def greet(self):
+        barrier = pltpu.get_barrier_semaphore()
+        for step in range(1, self.experts):
+            tell(barrier, self.peer(step)[1])
+        pl.when(self.row > 0)(lambda: tell(barrier, self.along(-1)))
+        pl.when(self.row < self.shards - 1)(lambda: tell(barrier, self.along(1)))
+        ends = jnp.where(self.row > 0, 1, 0) + jnp.where(self.row < self.shards - 1, 1, 0)
+        pl.semaphore_wait(barrier, self.experts - 1 + ends)
+
+
+def tell(semaphore, device):
+    pl.semaphore_signal(semaphore, inc=1, device_id=device, device_id_type=pl.DeviceIdType.MESH)
+
+
+def remote(src, dst, sent, came, device):
+    return pltpu.make_async_remote_copy(
+        src_ref=src, dst_ref=dst, send_sem=sent, recv_sem=came, device_id=device,
+        device_id_type=pl.DeviceIdType.MESH,
+    )
+
+
+def exchange_copies(place, send, recv, sent, came):
+    copies = []
+    for step in range(1, place.experts):
+        other, device = place.peer(step)
+        copies.append(remote(send.at[other], recv.at[place.member], sent.at[step], came.at[step], device))
+    own = pltpu.make_async_copy(send.at[place.member], recv.at[place.member], sent.at[0])
+    return [own, *copies]
+
+
+def placed(col_in, row_in, col_shape, row_shape):
     tokens = col_in.shape[0]
     down = lax.broadcasted_iota(jnp.int32, (tokens, tokens), 0)
     across = lax.broadcasted_iota(jnp.int32, (tokens, tokens), 1)
-    lanes = lax.broadcasted_iota(jnp.int32, col_out.shape, 1)
+    lanes = lax.broadcasted_iota(jnp.int32, col_shape, 1)
     named = (col_in[:, 0:1] == lanes) | (col_in[:, 1:2] == lanes)
     before = (across < down).astype(F32).astype(BF16)
     ranks = mm(before, named.astype(F32).astype(BF16))
-    col_out[...] = jnp.where(named, ranks, -1.0)
-    lines = lax.broadcasted_iota(jnp.int32, row_out.shape, 0)
+    col = jnp.where(named, ranks, -1.0)
+    lines = lax.broadcasted_iota(jnp.int32, row_shape, 0)
     named = (row_in[0:1, :] == lines) | (row_in[1:2, :] == lines)
     before = (down < across).astype(F32).astype(BF16)
     ranks = mm(named.astype(F32).astype(BF16), before)
-    row_out[...] = jnp.where(named, ranks, -1.0)
+    return col, jnp.where(named, ranks, -1.0)
 
 
 def chosen(row_ref, expert, slots):
     tokens = row_ref.shape[1]
     index = lax.broadcasted_iota(jnp.int32, (slots, tokens), 0).astype(F32)
-    return jnp.where(index == row_ref[pl.ds(expert, 1), :], 1.0, 0.0).astype(BF16)
+    return jnp.where(index == row_ref[expert : expert + 1, :], 1.0, 0.0).astype(BF16)
 
 
 def taken(col, expert, slots):
@@ -98,22 +163,123 @@
     return jnp.where(index == col[:, expert : expert + 1], 1.0, 0.0).astype(BF16)
 
 
-def dispatch_grads_kernel(cot, gates, routes, row, out):
-    experts, slots, _ = out.shape
+def ready_kernel(
+    images, real, parts,
+    x, cot, gates, routes, routes_row, mats, vecs, up, down, biases,
+    rows_in, grads_in, up_out, down_out, biases_out, middle_out, qkv, context, squares, full, rows_of, col,
+    send_grads, send_rows, row, vec_all, sent_g, came_g, sent_r, came_r, sent_p, came_p, sent_v, came_v,
+    sent_w, came_w,
+):
+    place = Place()
+    tokens, width = x.shape
+    lines = tokens // images
+    experts, slots, _ = send_rows.shape
+    shards = place.shards
+    place.greet()
+
+    share = mats.shape[0]
+    mine = pl.ds(place.shard * share, share)
+    partner = (place.expert, place.shard + 1 - 2 * place.core)
+    own = [
+        pltpu.make_async_copy(mats, full.at[mine], sent_p.at[0]),
+        pltpu.make_async_copy(vecs, vec_all.at[place.shard], sent_v.at[0]),
+    ]
+    for c in own:
+        c.start()
+    chips = []
+    for step in range(1, shards // 2):
+        there = (place.expert, lax.rem(place.chip + step, shards // 2) * 2 + place.core)
+        chips.append(remote(mats, full.at[mine], sent_p.at[step], came_p.at[step], there))
+        chips.append(remote(vecs, vec_all.at[place.shard], sent_v.at[step], came_v.at[step], there))
+    for c in chips:
+        c.start()
+
+    def pieces(k, here, there, sent, came, device):
+        wide = up.shape[1] // parts
+        cols, lots = pl.ds(k * wide, wide), pl.ds(k * wide, wide)
+        out = [
+            remote(here[0].at[:, cols], there[0].at[:, cols], sent.at[3 * k], came.at[3 * k], device),
+            remote(here[1].at[lots, :], there[1].at[lots, :], sent.at[3 * k + 1], came.at[3 * k + 1], device),
+        ]
+        if k == 0:
+            out.append(remote(here[2], there[2], sent.at[3 * k + 2], came.at[3 * k + 2], device))
+        return out
+
+    held, landed = (up, down, biases), (up_out, down_out, biases_out)
+    rightmost = place.shards - 1
+    local = [pltpu.make_async_copy(h, t, sent_w.at[2, i]) for i, (h, t) in enumerate(zip(held, landed))]
+
+    def matrices(k, source, way):
+        return pieces(k, source, landed, sent_w.at[(way + 1) // 2], came_w, place.along(way))
+
+    def start_all(copies):
+        for c in copies:
+            c.start()
+
+    @pl.when(place.row == place.root)
+    def _():
+        start_all(local)
+        for way, more in ((-1, place.row > 0), (1, place.row < rightmost)):
+
+            @pl.when(more)
+            def _(way=way):
+                for k in range(parts):
+                    start_all(matrices(k, held, way))
+
+    def pass_on(k):
+        @pl.when(place.row != place.root)
+        def _():
+            for c in matrices(k, landed, 1):
+                c.wait_recv()
+
+        for way, more in (
+            (-1, (place.row > 0) & (place.row < place.root)),
+            (1, (place.row < rightmost) & (place.row > place.root)),
+        ):
+
+            @pl.when(more)
+            def _(way=way):
+                start_all(matrices(k, landed, way))
+
+    col_all, row_all = placed(routes, routes_row, col.shape, row.shape)
+    col[...] = col_all
+    row[...] = row_all
     upstream = cot[...].astype(F32)
-    for e in range(experts):
+    for j in range(experts):
+        e = expert_of(j, experts, shards)
         gate = jnp.where(routes[:, 0:1] == e, gates[:, 0:1], 0.0) + jnp.where(
             routes[:, 1:2] == e, gates[:, 1:2], 0.0
         )
-        scaled = (upstream * gate).astype(BF16)
-        out[e] = mm(chosen(row, e, slots), scaled).astype(BF16)
-
-
-def forward_kernel(
-    images, real, x, w_in, w_out, gain, shift, bias, row, middle_out, qkv, context, send, squares, ctx_t
-):
-    tokens, width = x.shape
-    lines = tokens // images
+        send_grads[j] = mm(chosen(row, e, slots), (upstream * gate).astype(BF16)).astype(BF16)
+    swap_g = exchange_copies(place, send_grads, grads_in, sent_g, came_g)
+    start_all(swap_g)
+
+    over = []
+    for step in range(shards // 2):
+        source = lax.rem(place.chip + step, shards // 2) * 2 + place.core
+        block = pl.ds(source * share, share)
+        if step:
+            back = shards // 2 - step
+            chips[2 * back - 2].wait_recv()
+            chips[2 * back - 1].wait_recv()
+        else:
+            own[0].wait()
+            own[1].wait()
+        at = shards // 2 + step
+        over.append(remote(full.at[block], full.at[block], sent_p.at[at], came_p.at[at], partner))
+        over.append(remote(vec_all.at[source], vec_all.at[source], sent_v.at[at], came_v.at[at], partner))
+        over[-2].start()
+        over[-1].start()
+    for c in over:
+        c.wait_recv()
+    vectors = vec_all[0]
+    for s in range(1, shards):
+        vectors = vectors + vec_all[s]
+    rows_of[...] = vectors
+    gain, shift, bias = vectors[0:2], vectors[2:4], vectors[4:7]
+    w_in, w_out = full.at[:, : 3 * width], full.at[:, 3 * width :]
+    pass_on(0)
+
     stream = x[...].astype(F32)
     unit, _ = normalize(stream)
     normed = (unit * gain[0:1, :] + shift[0:1, :]).astype(BF16)
@@ -130,15 +296,15 @@
             q = qkv[rows, s * SLAB : (s + 1) * SLAB]
             k = qkv[rows, width + s * SLAB : width + (s + 1) * SLAB]
             v = qkv[rows, 2 * width + s * SLAB : 2 * width + (s + 1) * SLAB]
-            parts = []
+            heads = []
             for h in range(2):
                 keep = half if h == 0 else ~half
                 scores = mt(jnp.where(keep, k, jnp.zeros_like(k)), q) * (HEAD**-0.5)
                 scores = jnp.where(valid, scores, -1e30)
                 powers = jnp.exp(scores - jnp.max(scores, axis=0, keepdims=True))
                 soft = powers / jnp.sum(powers, axis=0, keepdims=True)
-                parts.append(tm(soft.astype(BF16), v))
-            context[rows, s * SLAB : (s + 1) * SLAB] = jnp.where(half, parts[0], parts[1]).astype(BF16)
+                heads.append(tm(soft.astype(BF16), v))
+            context[rows, s * SLAB : (s + 1) * SLAB] = jnp.where(half, heads[0], heads[1]).astype(BF16)
         return carry
 
     lax.fori_loop(0, images, one_image, 0)
@@ -146,13 +312,176 @@
     middle_out[...] = middle
     unit, _ = normalize(middle)
     normed = (unit * gain[1:2, :] + shift[1:2, :]).astype(BF16)
-    experts, slots, _ = send.shape
-    for e in range(experts):
-        send[e] = mm(chosen(row, e, slots), normed).astype(BF16)
+    for j in range(experts):
+        send_rows[j] = mm(chosen(row, expert_of(j, experts, shards), slots), normed).astype(BF16)
+    swap_r = exchange_copies(place, send_rows, rows_in, sent_r, came_r)
+    start_all(swap_r)
     index = lax.broadcasted_iota(jnp.int32, (tokens, 1), 0)
     counts = jnp.where(lax.rem(index, lines) < real, 1.0, 0.0)
     squares[0:1, :] = jnp.sum(stream * stream, axis=0, keepdims=True)
     squares[1:2, :] = jnp.sum(middle * middle * counts, axis=0, keepdims=True)
+
+    for k in range(1, parts):
+        pass_on(k)
+    for c in swap_g + swap_r:
+        c.wait()
+    for c in chips + over:
+        c.wait_send()
+
+    @pl.when(place.row == place.root)
+    def _():
+        for c in local:
+            c.wait()
+
+    for way, more in (
+        (-1, (place.row > 0) & (place.row <= place.root)),
+        (1, (place.row < rightmost) & (place.row >= place.root)),
+    ):
+
+        @pl.when(more)
+        def _(way=way):
+            for k in range(parts):
+                for c in matrices(k, landed, way):
+                    c.wait_send()
+
+
+def give_back_kernel(
+    parts, back, made, up, down, small,
+    back_out, made_out, up_out, down_out, small_out,
+    up_l, down_l, small_l, up_r, down_r, small_r,
+    sent_b, came_b, sent_m, came_m, sent_c, came_l, came_r, sent_d, came_d, sent_o, came_o,
+):
+    place = Place()
+    place.greet()
+    swap_b = exchange_copies(place, back, back_out, sent_b, came_b)
+    for c in swap_b:
+        c.start()
+    swap_m = exchange_copies(place, made, made_out, sent_m, came_m)
+    for c in swap_m:
+        c.start()
+    rightmost = place.shards - 1
+    row, root = place.row, place.root
+    own, out = (up, down, small), (up_out, down_out, small_out)
+    left, right = (up_l, down_l, small_l), (up_r, down_r, small_r)
+    heights = (up.shape[0] // parts, down.shape[0] // parts)
+
+    def piece(ref, i, k):
+        return ref if i == 2 else ref.at[pl.ds(k * heights[i], heights[i])]
+
+    def of(k):
+        return range(3) if k == 0 else range(2)
+
+    def hop(k, source, target, came, way):
+        return [
+            remote(piece(source[i], i, k), piece(target[i], i, k), sent_c.at[3 * k + i], came.at[3 * k + i], place.along(way))
+            for i in of(k)
+        ]
+
+    def add(k, target, terms):
+        for i in of(k):
+            total = piece(terms[0][i], i, k)[...].astype(F32)
+            for t in terms[1:]:
+                total += piece(t[i], i, k)[...].astype(F32)
+            piece(target[i], i, k)[...] = total.astype(target[i].dtype)
+
+    def wait_for(k, buffer, came):
+        for c in hop(k, buffer, buffer, came, 1):
+            c.wait_recv()
+
+    def go(copies):
+        for c in copies:
+            c.start()
+
+    def chain(k):
+        pl.when((row == 0) & (root > 0))(lambda: go(hop(k, own, left, came_l, 1)))
+        pl.when((row == rightmost) & (root < rightmost))(lambda: go(hop(k, own, right, came_r, -1)))
+
+        @pl.when((row > 0) & (row < root))
+        def _():
+            wait_for(k, left, came_l)
+            add(k, left, [own, left])
+            go(hop(k, left, left, came_l, 1))
+
+        @pl.when((row < rightmost) & (row > root))
+        def _():
+            wait_for(k, right, came_r)
+            add(k, right, [own, right])
+            go(hop(k, right, right, came_r, -1))
+
+        @pl.when((row == root) & (row > 0))
+        def _():
+            wait_for(k, left, came_l)
+            add(k, out, [own, left])
+
+        @pl.when((row == root) & (row == 0))
+        def _():
+            add(k, out, [own])
+
+        @pl.when((row == root) & (row < rightmost))
+        def _():
+            wait_for(k, right, came_r)
+            add(k, out, [out, right])
+
+        @pl.when(row == root)
+        def _():
+            for step in range(1, place.shards // 2):
+                go(spread(k, step))
+            go(cross(k))
+
+    root_core = jnp.where(row < place.shards // 2, 0, 1)
+    root_chip = jnp.where(row < place.shards // 2, row, place.shards - 1 - row)
+
+    def spread(k, step):
+        there = (place.expert, lax.rem(place.chip + step, place.shards // 2) * 2 + place.core)
+        at = lambda i: (step - 1, 3 * k + i)
+        return [
+            remote(piece(out[i], i, k), piece(out[i], i, k), sent_d.at[at(i)], came_d.at[3 * k + i], there) for i in of(k)
+        ]
+
+    def cross(k):
+        there = (place.expert, place.shard + 1 - 2 * place.core)
+        return [
+            remote(piece(out[i], i, k), piece(out[i], i, k), sent_o.at[3 * k + i], came_o.at[3 * k + i], there) for i in of(k)
+        ]
+
+    def hand_out(k):
+        @pl.when((place.core == root_core) & (place.chip != root_chip))
+        def _():
+            for c in spread(k, 1):
+                c.wait_recv()
+            go(cross(k))
+
+        @pl.when(place.core != root_core)
+        def _():
+            for c in cross(k):
+                c.wait_recv()
+
+    lag = 3
+    for k in range(parts + lag):
+        if k < parts:
+            chain(k)
+        if k >= lag:
+            hand_out(k - lag)
+    for k in range(parts):
+
+        @pl.when(row != root)
+        def _(k=k):
+            for c in hop(k, left, left, came_l, 1):
+                c.wait_send()
+
+        @pl.when(row == root)
+        def _(k=k):
+            for step in range(1, place.shards // 2):
+                for c in spread(k, step):
+                    c.wait_send()
+
+        @pl.when(place.core == root_core)
+        def _(k=k):
+            for c in cross(k):
+                c.wait_send()
+
+    for c in swap_b + swap_m:
+        c.wait()
 
 
 def expert_kernel(
@@ -194,7 +523,7 @@
 
 
 def backward_kernel(
-    images, real, x, w_in, w_out, gain, shift, qkv, context, middle, cot, col, back,
+    images, real, shards, x, w_in, w_out, gain, shift, qkv, context, middle, cot, col, back,
     d_x, d_in, d_out, d_gain, d_shift, d_bias, d_qkv, d_context,
 ):
     tokens, width = x.shape
@@ -202,7 +531,7 @@
     experts, slots, _ = back.shape
     back_two = jnp.zeros((tokens, width), F32)
     for e in range(experts):
-        back_two += mm(taken(col, e, slots), back[e])
+        back_two += mm(taken(col, expert_of(e, experts, shards), slots), back[e])
     unit, inverse = normalize(middle[...])
     d_gain[1:2, :] = jnp.sum(back_two * unit, axis=0, keepdims=True)
     d_shift[1:2, :] = jnp.sum(back_two, axis=0, keepdims=True)
@@ -253,14 +582,15 @@
     d_x[...] += normalize_back(back_one, unit, inverse, gain[0:1, :])
 
 
-def output_kernel(lines, real, middle, cot, gates, routes, col, returned, out, d_gates, squares):
+def output_kernel(lines, real, shards, middle, cot, gates, routes, col, returned, out, d_gates, squares):
     tokens, width = middle.shape
     experts, slots, _ = returned.shape
     rows = [jnp.zeros((tokens, width), F32) for _ in range(TOP)]
     for r in range(TOP):
-        for e in range(experts):
+        for j in range(experts):
+            e = expert_of(j, experts, shards)
             mine = jnp.where(routes[:, r : r + 1] == e, col[:, e : e + 1], -1.0)
-            rows[r] += mm(taken(mine, 0, slots), returned[e])
+            rows[r] += mm(taken(mine, 0, slots), returned[j])
     upstream = cot[...].astype(F32)
     total = middle[...]
     for r in range(TOP):
@@ -288,36 +618,41 @@
         wide = jnp.pad(values, ((0, 0), (0, lines - real), (0, 0)), constant_values=fill)
         return wide.reshape(tokens, values.shape[2])
 
-    matrices = jnp.concatenate([attention_in, attention_out], axis=1)
-    vectors = jnp.concatenate([layer_gain, layer_shift, attention_bias], axis=0)
-    matrices = lax.all_gather(matrices, "shard", axis=0, tiled=True)
-    vectors = lax.all_gather(vectors, "shard", axis=1, tiled=True).astype(F32)
-    full_in, full_out = matrices[:, : 3 * width], matrices[:, 3 * width :]
-    gain, shift, bias = vectors[0:2], vectors[2:4], vectors[4:7]
+    mats = jnp.concatenate([attention_in, attention_out], axis=1)
+    vectors = jnp.concatenate([layer_gain, layer_shift, attention_bias], axis=0).astype(F32)
+    vectors = lax.dynamic_update_slice(
+        jnp.zeros((8, width), F32), vectors, (0, lax.axis_index("shard") * vectors.shape[1])
+    )
+    biases = jnp.concatenate([hidden_bias, expert_bias], axis=1).astype(F32)
 
     x, cot = padded(images), padded(cotangent)
     route_col, gate_col = padded(routes, -1), padded(gates)
-    col, row = call(
-        place_kernel,
-        [((tokens, up_to(experts, 128)), F32), ((up_to(experts, 8), tokens), F32)],
-        [route_col, route_col.T],
-    )
     block = (experts, slots, width)
-    send_grads = call(dispatch_grads_kernel, [(block, BF16)], [cot, gate_col, route_col, row])[0]
-    exchange = functools.partial(
-        lax.all_to_all, axis_name="expert", split_axis=0, concat_axis=0, tiled=True
-    )
-    grads = exchange(send_grads)
-    middle, qkv, context, send_rows, squares = call(
-        functools.partial(forward_kernel, count, real),
+    parts = 4
+    dma = pltpu.SemaphoreType.DMA
+    rows, grads, up_held, down_held, bias_held, middle, qkv, context, squares, full, vecs, col = call(
+        functools.partial(ready_kernel, count, real, parts),
         [
-            ((tokens, width), F32), ((tokens, 3 * width), BF16), ((tokens, width), BF16), (block, BF16),
-            ((2, width), F32),
+            (block, BF16), (block, BF16), ((width, hidden_units), BF16), ((hidden_units, width), BF16),
+            ((1, hidden_units + width), F32), ((tokens, width), F32), ((tokens, 3 * width), BF16),
+            ((tokens, width), BF16), ((2, width), F32), ((width, 4 * width), BF16), ((8, width), F32),
+            ((tokens, up_to(experts, 128)), F32),
         ],
-        [x, full_in, full_out, gain, shift, bias, row],
-        [pltpu.VMEM((8, 128), F32)],
-    )
-    rows = exchange(send_rows)
+        [
+            x, cot, gate_col, route_col, route_col.T, mats, vectors, expert_up[0], expert_down[0], biases,
+        ],
+        [
+            pltpu.VMEM(block, BF16), pltpu.VMEM(block, BF16), pltpu.VMEM((up_to(experts, 8), tokens), F32),
+            pltpu.VMEM((shards, 8, width), F32),
+            dma((experts,)), dma((experts,)), dma((experts,)), dma((experts,)),
+            dma((shards,)), dma((shards,)), dma((shards,)), dma((shards,)),
+            dma((3, 3 * parts)), dma((3 * parts,)),
+        ],
+        outside=(7, 8, 9, 12, 13, 14),
+        collective=0,
+    )
+    full_in, full_out = full[:, : 3 * width], full[:, 3 * width :]
+    gain, shift, bias = vecs[0:2], vecs[2:4], vecs[4:7]
 
     every = experts * slots
     steps = 8
@@ -346,18 +681,28 @@
         scratch_shapes=[pltpu.VMEM((width, hidden_units), F32), pltpu.VMEM((width, hidden_units), F32)],
         compiler_params=pltpu.CompilerParams(vmem_limit_bytes=VMEM_LIMIT),
     )(
-        rows.reshape(every, width), grads.reshape(every, width), expert_up[0], hidden_bias.astype(F32),
-        expert_down[0], expert_bias.astype(F32),
-    )
-    routed = exchange(back.reshape(block))
-    returned = exchange(made.reshape(block))
-    up_total = lax.psum(d_up, "shard").astype(F32)
-    down_total = lax.psum(d_down, "shard").astype(F32)
-    small = jnp.concatenate([d_hidden, d_eb], axis=1).astype(BF16)
-    small = lax.psum(small, "shard").astype(F32)
+        rows.reshape(every, width), grads.reshape(every, width), up_held, bias_held[:, :hidden_units],
+        down_held, bias_held[:, hidden_units:],
+    )
+    small = jnp.concatenate([d_hidden, d_eb], axis=1)
+    parts = 8
+    matrix_shapes = [(d_up.shape, BF16), (d_down.shape, BF16), (small.shape, F32)]
+    routed, returned, up_total, down_total, small = call(
+        functools.partial(give_back_kernel, parts),
+        [(block, BF16), (block, BF16), *matrix_shapes],
+        [back.reshape(block), made.reshape(block), d_up, d_down, small],
+        [
+            *[pltpu.VMEM(s, d) for s, d in 2 * matrix_shapes],
+            dma((experts,)), dma((experts,)), dma((experts,)), dma((experts,)),
+            dma((3 * parts,)), dma((3 * parts,)), dma((3 * parts,)),
+            dma((shards // 2, 3 * parts)), dma((3 * parts,)), dma((3 * parts,)), dma((3 * parts,)),
+        ],
+        collective=1,
+    )
+    up_total, down_total = up_total.astype(F32), down_total.astype(F32)
 
     d_x, d_in, d_out, d_gain, d_shift, d_bias = call(
-        functools.partial(backward_kernel, count, real),
+        functools.partial(backward_kernel, count, real, shards),
         [
             ((tokens, width), F32), ((width, 3 * width), BF16), ((width, width), BF16), ((2, width), F32),
             ((2, width), F32), ((3, width), F32),
@@ -366,7 +711,7 @@
         [pltpu.VMEM((tokens, 3 * width), BF16), pltpu.VMEM((tokens, width), BF16)],
     )
     block_output, d_gates, last = call(
-        functools.partial(output_kernel, lines, real),
+        functools.partial(output_kernel, lines, real, shards),
         [((tokens, width), BF16), ((tokens, TOP), F32), ((1, width), F32)],
         [middle, cot, gate_col, route_col, col, returned],
     )

time: 574 us -> 575 us (level)
  Pallas kernels: 134 us -> 394 us
  waiting for transfers between devices: 225 us -> 70 us
  blocking collectives: 134 us -> 50.2 us
  starting transfers between devices: 15.9 us -> 0.33 us
    pallas_call x5 -> x4, Pallas kernels: 65.2 us -> 325 us  [call(): pl.pallas_call(body, out_shape=[jax.ShapeDtypeStruct(s, d) for s, d in ou...]
    all_to_all x3 -> x0, waiting for transfers between devices: 98.2 us -> none  [the longest x1 71.6 us: local(): rows = exchange(send_rows)]
    all_to_all x1 -> x0, blocking collectives: 78.2 us -> none  [local(): routed = exchange(back.reshape(block))]
    psum x1 -> x0, waiting for transfers between devices: 76.1 us -> none  [local(): up_total = lax.psum(d_up, 'shard').astype(F32)]
    psum x1, waiting for transfers between devices: 8.25 us -> 69.9 us  [local(): owned = lax.psum(owned, 'expert').astype(F32)]
    reduce_scatter x1, waiting for transfers between devices: 26.3 us -> 0.01 us  [local(): owned = lax.psum_scatter(owned, 'shard', scatter_dimension=0, tiled=True)]
    all_gather x1 -> x0, waiting for transfers between devices: 15.8 us -> none  [local(): matrices = lax.all_gather(matrices, 'shard', axis=0, tiled=True)]
    all_to_all x3 -> x0, starting transfers between devices: 15.5 us -> none  [the longest x1 7.42 us: local(): grads = exchange(send_grads)]
  transfers between devices with their start and end apart: 7 -> 2, of which waited for: 6 -> 1; matrix products, arithmetic and copies ran while one was open for 5% -> 2% of each run, Pallas kernels for 5% -> 2%
where the time goes in v2:
time: 575 us; the launch traced here: 570 us
  Pallas kernels  394 us (69%)
  waiting for transfers between devices  70 us (12%)
  blocking collectives  50.2 us (9%)
  local copies, waits for them, and re-layouts  25.5 us (4%)
  other arithmetic  15.7 us (3%)
  between operations  14.8 us (3%)
    pallas_call x4, Pallas kernels, call(): pl.pallas_call(body, out_shape=[jax.ShapeDtypeStruct(s, d) for s, d in ou...  325 us
    psum x1, waiting for transfers between devices, local(): owned = lax.psum(owned, 'expert').astype(F32)  69.9 us
    pallas_call x1, Pallas kernels, local(): pl.pallas_call(functools.partial(expert_kernel, 512), grid=(steps,), out_...  69.2 us
    psum x1, blocking collectives, local(): sums = lax.psum(sums, ('expert', 'shard'))  50.2 us
  transfers between devices with their start and end apart: 2, of which 1 were waited for; matrix products, arithmetic and copies ran while one was open for 2% of the time, Pallas kernels for 2%

profile of v2, /device:TPU:0, one launch (start us, length us, event | category | flops | bytes accessed | tf_op | source)
XLA Modules:
  0.0 570.2 jit_solution(8029452690492213438)
XLA Ops:
  7.2 1.0 copy.44
  8.3 0.8 copy.30.routes_row
  9.1 0.9 copy.43
  10.0 0.1 copy.41
  10.2 0.1 copy.42
  10.4 1.0 pad.23.clone
  11.4 1.0 pad.24.clone
  12.4 0.6 maximum_convert_fusion.biases
  13.0 0.8 pad.25.clone
  13.8 0.8 pad_maximum_fusion.mats
  14.7 0.4 dynamic_update_slice.3.vecs
  15.1 0.6 copy-done.10
  15.7 140.2 %shard_map.228 = (bf16[8,400,512]{2,1,0:T(8,128)(2,1)}, bf16[8,400,512]{2,1,0:T(8,128)(2,1)}, bf16[512,2048]{1,0:T(8,128)(2,1)}, bf16[2048,512]{1,0:T(8,128)(2,1...) custom-call(bf16[832,512]{1,0:T(8,128)(2,1)} %bitcast.28, ...), custom_call_target="tpu_custom_call" | custom-call | tf_op jit(solution)/shard_map/pallas_call | solution.py:65
  156.0 1.3 slice.52.out_bias
  157.3 1.3 slice.51.hidden_bias
  158.6 1.9 slice.55.w_out
  160.4 2.7 slice.54.w_in
  163.1 0.6 fusion.9
  163.7 69.2 %shard_map.229 = (bf16[3200,512]{1,0:T(8,128)(2,1)}, bf16[3200,512]{1,0:T(8,128)(2,1)}, bf16[512,2048]{1,0:T(8,128)(2,1)}, f32[1,2048]{1,0:T(1,128)}, bf16[2048,512]{1,0:T(8,128)(2,1)}, /*index=5*/f32[1,512]{1,0:T(1,128)}) custom-call(bf16[3200,512]{1,0:T(8,128)(2,1)} %bitcast.35, bf16[3200,512]{1,0:T(8,128)(2,1)} %bitcast.36, ...), custom_call_target="tpu_custom_call" | custom-call | tf_op jit(solution)/shard_map/pallas_call | solution.py:662
  232.8 1.3 pad_maximum_fusion.1.small
  234.2 144.0 %shard_map.230 = (bf16[8,400,512]{2,1,0:T(8,128)(2,1)}, bf16[8,400,512]{2,1,0:T(8,128)(2,1)}, bf16[512,2048]{1,0:T(8,128)(2,1)}, bf16[2048,512]{1,0:T(8,128)(2,1)}, f32[1,2560]{1,0:T(1,128)}) custom-call(bf16[8,400,512]{2,1,0:T(8,128)(2,1)} %bitcast.38, bf16[8,400,512]{2,1,0:T(8,128)(2,1)} %bitcast.37, bf16[512,2048]{1,0:T(8,128)(2,1)} %get-tuple-element.54.up, ...), custom_call_target="tpu_custom_call" | custom-call | tf_op jit(solution)/shard_map/pallas_call | solution.py:65
  378.2 28.2 %shard_map.232 = (f32[832,512]{1,0:T(8,128)}, bf16[512,1536]{1,0:T(8,128)(2,1)}, bf16[512,512]{1,0:T(8,128)(2,1)}, f32[2,512]{1,0:T(2,128)}, f32[2,512]{1,0:T(2,128)}, /*index=5*/f32[3,512]{1,0:T(4,128)}) custom-call(bf16[832,512]{1,0:T(8,128)(2,1)} %bitcast.29, bf16[512,1536]{1,0:T(8,128)(2,1)} %slice.54.w_in, bf16[512,512]{1,0:T(8,128)(2,1)} %slice.55.w_out, ...), custom_call_target="tpu_custom_call" | custom-call | tf_op jit(solution)/shard_map/pallas_call | solution.py:65
  406.4 0.7 convert.11
  407.0 0.7 convert.12
  407.7 0.7 convert.13
  408.5 0.2 copy.45
  408.6 3.1 fusion.1
  411.8 0.3 all-reduce.8.cloned.1.call-start
  412.1 12.2 %shard_map.231 = (bf16[832,512]{1,0:T(8,128)(2,1)}, f32[832,2]{1,0:T(8,128)}, f32[1,512]{1,0:T(1,128)}) custom-call(f32[832,512]{1,0:T(8,128)} %get-tuple-element.45.middle, bf16[832,512]{1,0:T(8,128)(2,1)} %bitcast.27, f32[832,2]{1,0:T(8,128)} %bitcast.34, s32[832,2]{1,0:T(8,128)} %bitcast.32, f32[832,128]{1,0:T(8,128)} %get-tuple-element.46.col, ...), custom_call_target="tpu_custom_call" | custom-call | tf_op jit(solution)/shard_map/pallas_call | solution.py:65
  424.2 0.9 maximum_reduce_fusion
  425.1 50.2 %psum.15 = f32[3]{0:T(128)S(1)} all-reduce(f32[3]{0:T(128)S(1)} %maximum_reduce_fusion), channel_id=1, replica_groups=mesh['expert'=8,'shard'=4] {'expert','shard'}, use_global_device_ids=true, to_apply=%region_3.4 | all-reduce | flops 3 | bytes 24 | tf_op jit(solution)/shard_map/psum | solution.py:719
  475.3 0.6 slice.66
  475.9 0.6 slice.65
  476.5 1.3 slice.68
  477.8 1.3 copy.38
  479.1 0.8 copy.40
  479.9 0.1 slice.69
  480.1 2.2 copy.39
  482.3 0.5 multiply_sqrt_fusion
  482.8 2.5 bitcast_convert_fusion.1
  485.4 2.6 bitcast_convert_fusion
  488.0 69.9 %all-reduce.8.cloned.1.call-done = bf16[128,2176]{1,0:T(8,128)(2,1)} async-done(((bf16[128,2176]{1,0:T(8,128)(2,1)}), bf16[128,2176]{1,0:T(8,128)(2,1)}) %all-reduce.8.cloned.1.call-update) | async-done | bytes 557072 | tf_op jit(solution)/shard_map/psum | solution.py:726
  557.9 1.2 convert_element_type.23
  559.3 0.7 copy.37
  559.9 0.6 copy.36
  560.6 0.6 copy.35
  561.2 0.7 slice.71
  561.9 1.0 slice.70
  (49 shorter events, 0.4 us)
Async XLA Ops:
  7.2 2.8 copy-start.5
  7.2 2.9 copy-start.6
  7.2 478.1 %reduce-scatter.2.cloned.1.call-start = ((), (), s32[]{:S(2)}) async-start(), calls=%async_computation.1 | async-start | bytes 2785280 | tf_op jit(solution)/shard_map/reduce_scatter | solution.py:725
  8.3 3.1 copy-start
  10.1 2.3 copy-start.12
  10.2 2.3 copy-start.15
  10.3 3.5 copy-start.8
  10.3 3.5 copy-start.9
  10.3 4.3 copy-start.16
  10.4 4.3 copy-start.17
  10.4 4.3 copy-start.18
  15.1 0.6 copy-start.10
  156.0 7.1 %copy-start.13 = (f32[8,512]{1,0:T(8,128)S(1)}, f32[8,512]{1,0:T(8,128)}, u32[]{:S(2)}) copy-start(f32[8,512]{1,0:T(8,128)} %get-tuple-element.61) | copy-start | bytes 49156
  411.8 146.2 %all-reduce.8.cloned.1.call-start = ((), (), s32[]{:S(2)}) async-start(), calls=%async_computation.2 | async-start | bytes 1114112 | tf_op jit(solution)/shard_map/psum | solution.py:726
  412.1 12.2 %copy-start.14 = (f32[2,512]{1,0:T(2,128)S(1)}, f32[2,512]{1,0:T(2,128)}, u32[]{:S(2)}) copy-start(f32[2,512]{1,0:T(2,128)} %get-tuple-element.75) | copy-start | bytes 12292
  412.1 63.2 %copy-start.11 = (f32[1,2560]{1,0:T(1,128)S(1)}, f32[1,2560]{1,0:T(1,128)}, u32[]{:S(2)}) copy-start(f32[1,2560]{1,0:T(1,128)} %get-tuple-element.72) | copy-start | bytes 30724
  424.2 54.9 %copy-start.7 = (f32[832,2]{1,0:T(8,128)S(1)}, f32[832,2]{1,0:T(8,128)}, u32[]{:S(2)}) copy-start(f32[832,2]{1,0:T(8,128)} %get-tuple-element.74) | copy-start | bytes 19972
  476.5 3.5 copy-start.4
  480.1 2.7 copy-start.3
  482.8 2.6 copy-start.2
  557.9 3.3 copy-start.1
Sparse Core Ops, SparseCore 0:
  411.9 41.8 reduce-scatter.1
  485.5 72.3 all-reduce.7
